TPU v7x, 32 devices: a whole 2x2x4 slice. The times are simulated.
32 devices in a mesh: clip: 16 (over z, y, x), frame: 2 (over core).
Axes of the slice: x: 2, y: 2, z: 4, core: 2. Of those that a mesh axis runs over, the one named last changes fastest.
Arguments:
- clip_tokens: bfloat16 [16, 8, 196, 768], P('clip', 'frame'), may hold values from -6 to 6
- clip_class: bfloat16 [16, 768], P('clip'), may hold values from -6 to 6
- output_grad: bfloat16 [16, 8, 196, 768], P('clip', 'frame'), may hold values from -6 to 6
- class_grad: bfloat16 [16, 768], P('clip'), may hold values from -6 to 6
- clip_count: int32 [16], P('clip'), may hold values from 1 to 1, as said below
- time_qkv: bfloat16 [768, 2304], P(('clip', 'frame')), may hold values from -0.21875 to 0.21875
- time_proj: bfloat16 [768, 768], P(('clip', 'frame')), may hold values from -0.625 to 0.625
- time_vec: bfloat16 [5, 768], P(None, ('clip', 'frame'))
- space_qkv: bfloat16 [768, 2304], P(('clip', 'frame')), may hold values from -0.21875 to 0.21875
- space_proj: bfloat16 [768, 768], P(('clip', 'frame')), may hold values from -1.25 to 1.25
- space_vec: bfloat16 [5, 768], P(None, ('clip', 'frame'))
- mlp_up: bfloat16 [768, 3072], P(('clip', 'frame')), may hold values from -0.21875 to 0.21875
- mlp_down: bfloat16 [3072, 768], P(('clip', 'frame')), may hold values from -0.109375 to 0.109375
- mlp_vec: bfloat16 [3, 768], P(None, ('clip', 'frame'))
- mlp_bias: bfloat16 [3072], P(('clip', 'frame')), may hold values from -3 to 3
Outputs:
- block_out: bfloat16 [16, 8, 196, 768], P('clip', 'frame')
- class_out: bfloat16 [16, 768], P('clip')
- token_grad: float32 [16, 8, 196, 768], P('clip', 'frame')
- class_in_grad: float32 [16, 768], P('clip')
- grad_time_qkv: float32 [768, 2304], P(('clip', 'frame'))
- grad_time_proj: float32 [768, 768], P(('clip', 'frame'))
- grad_time_vec: float32 [5, 768], P(None, ('clip', 'frame'))
- grad_space_qkv: float32 [768, 2304], P(('clip', 'frame'))
- grad_space_proj: float32 [768, 768], P(('clip', 'frame'))
- grad_space_vec: float32 [5, 768], P(None, ('clip', 'frame'))
- grad_mlp_up: float32 [768, 3072], P(('clip', 'frame'))
- grad_mlp_down: float32 [3072, 768], P(('clip', 'frame'))
- grad_mlp_vec: float32 [3, 768], P(None, ('clip', 'frame'))
- grad_mlp_bias: float32 [3072], P(('clip', 'frame'))
Inputs may be any that keep to these rules, and one draw needn't show every extreme that they name: Clip slot s of index i of clip is live when s < clip_count[i]; with one slot per index, every clip_count is 1 and every slot is live.
All inputs are finite; a program needn't handle non-finite values.
Results may differ from a plain program's by a relative error of at most 0.015.
Values may be sent and summed in bfloat16 or wider, within the bound.
No kernel may reach another device: no remote copies, remote signals or barrier semaphores. Data moves between devices by JAX's collectives and lax.ppermute only.
A program may use at most 192 MiB of HBM per device.

v0:
```python
import functools

import jax
import jax.numpy as jnp
from jax import lax
from jax.experimental import pallas as pl
from jax.experimental.pallas import tpu as pltpu
from jax.sharding import PartitionSpec as P

HEAD_DIM = 64
EPSILON = 1e-06
FLOAT = jnp.float32
BRAIN = jnp.bfloat16
LANES = 128
BLOCKS = 16
RATE = 1e9
VMEM_BYTES = 60 * 1024 * 1024


def nn(left, right):
    return lax.dot_general(left, right, (((1,), (0,)), ((), ())), preferred_element_type=FLOAT)


def nt(left, right):
    return lax.dot_general(left, right, (((1,), (1,)), ((), ())), preferred_element_type=FLOAT)


def tn(left, right):
    return lax.dot_general(left, right, (((0,), (0,)), ((), ())), preferred_element_type=FLOAT)


def unit_of(values):
    average = jnp.mean(values, axis=-1, keepdims=True)
    centred = values - average
    spread = jnp.mean(centred * centred, axis=-1, keepdims=True)
    inverse = lax.rsqrt(spread + EPSILON)
    return centred * inverse, inverse


def norm_back(unit, inverse, gain, upstream):
    scaled = upstream * gain
    inner = jnp.mean(scaled, axis=-1, keepdims=True)
    along = jnp.mean(scaled * unit, axis=-1, keepdims=True)
    return inverse * (scaled - inner - unit * along)


def column_sum(values):
    return jnp.sum(values, axis=0, keepdims=True)


def row_index(shape):
    return lax.broadcasted_iota(jnp.int32, shape, 0)


def head_map(width, first=0):
    lane = lax.broadcasted_iota(jnp.int32, (width, LANES), 0) // HEAD_DIM + first
    head = lax.broadcasted_iota(jnp.int32, (width, LANES), 1)
    return (lane == head).astype(FLOAT).astype(BRAIN)


def head_spread(width, first=0):
    head = lax.broadcasted_iota(jnp.int32, (LANES, width), 0)
    lane = lax.broadcasted_iota(jnp.int32, (LANES, width), 1) // HEAD_DIM + first
    return (lane == head).astype(FLOAT).astype(BRAIN)


def column_copies(core, mine, other, held, sems):
    half = held.shape[1] // 2
    copies = []
    for n, (source, slot) in enumerate(((mine, core), (other, 1 - core))):
        target = held.at[:, pl.ds(pl.multiple_of(slot * half, LANES), half)]
        copies.append(pltpu.make_async_copy(source.at[:, :half], target, sems.at[n]))
    return copies


def mlp_copies(core, plane, mine, other, up, down, sems):
    cut = up.shape[3]
    ups, downs = [], []
    for k, (sources, slot) in enumerate(((mine, core), (other, 1 - core))):
        for n, source in enumerate(sources):
            if len(sources) == 1:
                at, tail = (), (slice(None),)
            else:
                at, tail = ((slice(None), slice(0, 2), slice(2, 4))[max(n - 2, 0)], plane ^ min(n, 3)), ()
            rows = lambda low, high: source.at[(slice(None),) + tail + (slice(low, high),)]
            for t in (0, 1):
                part = up.at[(2 * slot + t,) + at]
                ups.append(pltpu.make_async_copy(rows(t * cut, (t + 1) * cut), part, sems.at[k, 3 * n + t]))
            part = down.at[at + (slot,)] if at else down.at[:, :, slot]
            downs.append(pltpu.make_async_copy(rows(2 * cut, 4 * cut), part, sems.at[k, 3 * n + 2]))
    return ups, downs


def start_first(copies):
    @pl.when(pl.program_id(0) == 0)
    def _():
        for copy in copies:
            copy.start()


def wait_first(copies):
    @pl.when(pl.program_id(0) == 0)
    def _():
        for copy in copies:
            copy.wait()


def merged(ref):
    return ref[...].reshape(ref.shape[0] * ref.shape[1], ref.shape[2])


def store(ref, value):
    ref[...] = value.astype(ref.dtype).reshape(ref.shape)


def marks(count, rows, low, high):
    index = row_index((count * rows, 1))
    found = (index >= low) & (index < high)
    for n in range(1, count):
        found = found | ((index >= n * rows + low) & (index < n * rows + high))
    return found


def time_mix_kernel(own_steps, info, tokens, far_tokens, vectors, w_mine, w_other, q_out, k_out, v_out, low_out, held, sems):
    step = pl.program_id(0)
    width = tokens.shape[-1]

    copies = column_copies(info[0], w_mine, w_other, held, sems)
    start_first(copies)
    unit, _ = unit_of(jnp.where(step < own_steps, merged(tokens).astype(FLOAT), merged(far_tokens).astype(FLOAT)))
    low = (unit * vectors[0:1] + vectors[1:2]).astype(BRAIN)
    wait_first(copies)
    store(k_out, nn(low, held[:, width : 2 * width]))
    store(v_out, nn(low, held[:, 2 * width :]) + vectors[3:4])

    @pl.when(step < own_steps)
    def _():
        queries = (nn(low, held[:, :width]) + vectors[2:3]).astype(BRAIN)
        store(q_out, queries * jnp.asarray(HEAD_DIM ** (-0.5), BRAIN))
        store(low_out, low)


def tree_sum(values):
    values = list(values)
    while len(values) > 1:
        values = [a + b for a, b in zip(values[::2], values[1::2])] + values[len(values) & ~1 :]
    return values[0]


def attention_kernel(
    places_here, info, tokens, vectors, q_in, k_in, v_in, begin, sw_mine, sw_other,
    prob_out, att_out, after_out, low_out, mixed_out, sprob_out, satt_out, places_out, class_out,
    held, sems,
):
    step = pl.program_id(0)
    frames = k_in.shape[0]
    count, rows, width = tokens.shape
    core = info[0]

    copies = column_copies(core, sw_mine, sw_other, held, sems)
    start_first(copies)
    mapping = head_map(width)
    spread = head_spread(width)
    for n in range(count):
        queries = q_in[n]
        scores = [nn(queries * k_in[g], mapping) for g in range(frames)]
        top = functools.reduce(jnp.maximum, scores)
        powers = [jnp.exp(s - top) for s in scores]
        scale = 1.0 / sum(powers)
        parts = []
        for g in range(frames):
            prob = (powers[g] * scale).astype(BRAIN)
            prob_out[n, g] = prob
            parts.append(nn(prob, spread).astype(BRAIN) * v_in[g])
        att_out[n] = tree_sum(parts)
    wait_first(copies)
    attended = merged(att_out)
    place = marks(count, rows, 0, places_here)
    base = merged(tokens).astype(FLOAT)
    after = jnp.where(place, base + (nn(attended, held[:, 4 * width :]) + vectors[4:5]), base)
    store(after_out, after)
    unit, _ = unit_of(after)
    low = (unit * vectors[5:6] + vectors[6:7]).astype(BRAIN)
    store(low_out, low)
    shape = (count, rows, width)
    queries = (nn(low, held[:, :width]) + vectors[7:8]).astype(BRAIN) * jnp.asarray(HEAD_DIM ** (-0.5), BRAIN)
    mixed_out[:, :, :width] = queries.reshape(shape)
    mixed_out[:, :, width : 2 * width] = nn(low, held[:, width : 2 * width]).astype(BRAIN).reshape(shape)
    mixed_out[:, :, 2 * width :] = (
        (nn(low, held[:, 2 * width : 3 * width]) + vectors[8:9]).astype(BRAIN).reshape(shape)
    )
    lane = lax.broadcasted_iota(jnp.int32, (1, LANES), 1)
    masks = [(lane // HEAD_DIM == e).astype(FLOAT).astype(BRAIN) for e in (0, 1)]
    key_ok = row_index((rows, 1)) <= places_here
    for n in range(count):
        for pair in range(width // LANES):
            at = pair * LANES
            q2 = mixed_out[n, :, at : at + LANES]
            k2 = mixed_out[n, :, width + at : width + at + LANES]
            v2 = mixed_out[n, :, 2 * width + at : 2 * width + at + LANES]
            result = []
            for e in (0, 1):
                logits = jnp.where(key_ok, nt(k2, q2 * masks[e]), -1e30)
                power = jnp.exp(logits - jnp.max(logits, axis=0, keepdims=True))
                prob = (power * (1.0 / jnp.sum(power, axis=0, keepdims=True))).astype(BRAIN)
                sprob_out[n, 2 * pair + e] = prob
                result.append(tn(prob, v2))
            satt_out[n, :, at : at + LANES] = jnp.where(lane < HEAD_DIM, result[0], result[1]).astype(BRAIN)
    spatial = nn(merged(satt_out), held[:, 3 * width : 4 * width]) + vectors[9:10]
    store(places_out, jnp.where(place, after, 0.0) + spatial)

    @pl.when(step == 0)
    def _():
        class_out[...] = begin[...]

    class_row = column_sum(jnp.where(marks(count, rows, places_here, places_here + 1), spatial, 0.0))
    class_out[0:1] = class_out[0:1] + class_row


def gelu_parts(values):
    half = 0.5 + 0.5 * lax.erf(values * (0.5 ** 0.5))
    density = jnp.exp(values * values * (-0.5)) * (0.5 / 3.141592653589793) ** 0.5
    return values * half, half + values * density


def mlp_kernel(
    places_here, all_frames, pieces, info, alive, places, grads, class_row, class_own, class_far, vectors, bias,
    *others,
):
    mine, other, others = others[:pieces], others[pieces : 2 * pieces], others[2 * pieces :]
    out, class_out, low_out, hidden_out, feed_out, before_out, rows_out, sums, slopes, up, down, sems = others
    step = pl.program_id(0)
    count, rows, width = places.shape
    core = info[0]

    ups, downs = mlp_copies(core, info[3], mine, other, up, down, sems)
    start_first(ups + downs)

    @pl.when(step == 0)
    def _():
        sums[...] = jnp.zeros_like(sums)

    class_mid = class_row[0:1] + (class_own[0:1] + class_far[0:1]) * all_frames ** (-0.5)
    last = (count - 1) * rows + places_here
    is_class = (row_index((count * rows, 1)) == last) & (step == pl.num_programs(0) - 1)
    kept = jnp.logical_not(marks(count, rows, places_here, places_here + 1) & (info[1] == 0))
    values = jnp.where(is_class, class_mid, merged(places))
    unit, inverse = unit_of(values)
    low = (unit * vectors[10:11] + vectors[11:12]).astype(BRAIN)
    store(low_out, low)
    feed = jnp.zeros((count * rows, width), FLOAT)
    chunks = hidden_out.shape[-1] // width
    wait_first(ups)
    for j in range(chunks):
        before = nn(low, up[j].reshape(width, width)) + bias[j : j + 1]
        hidden, slope = gelu_parts(before)
        hidden = hidden.astype(BRAIN)
        hidden_out[:, :, j * width : (j + 1) * width] = hidden.reshape(count, rows, width)
        slopes[j] = slope
        if j == 0:
            wait_first(downs)
        feed = feed + nn(hidden, down[j].reshape(width, width))
    result = ((values + (feed + vectors[12:13])) * alive[0]).reshape(count, rows, width)
    out[...] = result[:, :places_here].astype(BRAIN)
    class_out[...] = result[count - 1, places_here - places_here % 8 : places_here - places_here % 8 + 8]

    row_grad = merged(grads).astype(FLOAT) * alive[0]
    feed_grad = row_grad.astype(BRAIN)
    feed_kept = jnp.where(kept, row_grad, 0.0).astype(BRAIN)
    store(feed_out, feed_kept)
    sums[2:3] = sums[2:3] + column_sum(feed_kept.astype(FLOAT))
    upstream = jnp.zeros((count * rows, width), FLOAT)
    for j in range(chunks):
        hidden_grad = nt(feed_grad, down[j].reshape(width, width))
        before_grad = (hidden_grad * slopes[j]).astype(BRAIN)
        before_kept = jnp.where(kept, before_grad.astype(FLOAT), 0.0)
        before_out[:, :, j * width : (j + 1) * width] = before_kept.astype(BRAIN).reshape(count, rows, width)
        sums[3 + j : 4 + j] = sums[3 + j : 4 + j] + column_sum(before_kept)
        upstream = upstream + nt(before_grad, up[j].reshape(width, width))
    store(rows_out, row_grad + norm_back(unit, inverse, vectors[10:11], upstream))
    upstream = jnp.where(kept, upstream, 0.0)
    sums[0:1] = sums[0:1] + column_sum(upstream * unit)
    sums[1:2] = sums[1:2] + column_sum(upstream)


def space_back_kernel(
    places_here, all_frames, info, rows_grad, class_grad, after, mixed, sprob, satt, vectors, begin,
    sw_mine, sw_other,
    branch_out, mixed_out, after_out, time_out, att_out, sums, held, sems,
):
    step = pl.program_id(0)
    count, rows, width = after.shape
    core = info[0]

    copies = column_copies(core, sw_mine, sw_other, held, sems)
    start_first(copies)

    @pl.when(step == 0)
    def _():
        sums[...] = begin[...]

    place = marks(count, rows, 0, places_here)
    class_at = marks(count, rows, places_here, places_here + 1)
    offset = places_here % 16
    share = class_grad[0, offset : offset + 1] * all_frames ** (-0.5)
    direct = jnp.where(place, merged(rows_grad), 0.0)
    branch = jnp.where(class_at, share, direct).astype(BRAIN)
    store(branch_out, branch)
    sums[4:5] = sums[4:5] + column_sum(branch.astype(FLOAT))
    unit, inverse = unit_of(merged(after))
    wait_first(copies)
    att_grad = nt(branch, held[:, 3 * width : 4 * width]).astype(BRAIN)
    store(att_out, att_grad)
    spread = head_spread(width)
    lane = lax.broadcasted_iota(jnp.int32, (1, LANES), 1)
    masks = [(lane // HEAD_DIM == e).astype(FLOAT).astype(BRAIN) for e in (0, 1)]
    left = lane < HEAD_DIM
    for n in range(count):
        product = att_out[n].astype(FLOAT) * satt[n].astype(FLOAT)
        high = product.astype(BRAIN)
        rowdots = nt(spread, high) + nt(spread, (product - high.astype(FLOAT)).astype(BRAIN))
        for pair in range(width // LANES):
            at = pair * LANES
            a2 = att_out[n, :, at : at + LANES]
            q2 = mixed[n, :, at : at + LANES]
            k2 = mixed[n, :, width + at : width + at + LANES]
            v2 = mixed[n, :, 2 * width + at : 2 * width + at + LANES]
            queries, key_rows, value_rows = [], [], []
            for e in (0, 1):
                head = 2 * pair + e
                prob = sprob[n, head]
                prob_grad = nt(v2, a2 * masks[e])
                score = (prob.astype(FLOAT) * (prob_grad - rowdots[head : head + 1])).astype(BRAIN)
                queries.append(tn(score, k2))
                key_rows.append(nn(score, q2))
                value_rows.append(nn(prob, a2))
            q_grad = (jnp.where(left, queries[0], queries[1]) * HEAD_DIM ** (-0.5)).astype(BRAIN)
            k_grad = jnp.where(left, key_rows[0], key_rows[1]).astype(BRAIN)
            v_grad = jnp.where(left, value_rows[0], value_rows[1]).astype(BRAIN)
            mixed_out[n, :, at : at + LANES] = q_grad
            mixed_out[n, :, width + at : width + at + LANES] = k_grad
            mixed_out[n, :, 2 * width + at : 2 * width + at + LANES] = v_grad
    mixed_grad = merged(mixed_out)
    sums[2:3] = sums[2:3] + column_sum(mixed_grad[:, :width].astype(FLOAT))
    sums[3:4] = sums[3:4] + column_sum(mixed_grad[:, 2 * width :].astype(FLOAT))
    upstream = nt(mixed_grad, held[:, : 3 * width])
    inner = norm_back(unit, inverse, vectors[5:6], upstream)
    sums[0:1] = sums[0:1] + column_sum(upstream * unit)
    sums[1:2] = sums[1:2] + column_sum(upstream)
    sums[6:7] = sums[6:7] + column_sum(jnp.where(class_at, inner, 0.0))
    after_grad = jnp.where(place, direct + inner, 0.0)
    store(after_out, after_grad)
    low = after_grad.astype(BRAIN)
    store(time_out, low)
    sums[5:6] = sums[5:6] + column_sum(low.astype(FLOAT))
    store(att_out, nt(low, held[:, 4 * width :]))


def time_back_kernel(q_in, k_in, v_in, prob_in, att_in, q_out, own_out, far_out):
    own, rows, width = q_in.shape
    frames = k_in.shape[0]
    first = pl.program_id(0) * (width // HEAD_DIM)
    mapping = head_map(width, first)
    spread = head_spread(width, first)
    size = 16

    def chunk(index, carry):
        at = pl.ds(pl.multiple_of(index * size, size), size)
        values = [v_in[g, at] for g in range(frames)]
        att = [att_in[f, at] for f in range(own)]
        products = jnp.concatenate([att[f] * values[g] for f in range(own) for g in range(frames)], axis=0)
        prob_grad = nn(products, mapping)
        probs = [prob_in[f, g, at] for f in range(own) for g in range(frames)]
        scores = []
        for f in range(own):
            wide = [probs[f * frames + g].astype(FLOAT) for g in range(frames)]
            weighted = [
                wide[g] * prob_grad[(f * frames + g) * size : (f * frames + g + 1) * size] for g in range(frames)
            ]
            rowdot = sum(weighted)
            scores += [(weighted[g] - wide[g] * rowdot).astype(BRAIN) for g in range(frames)]
        score_wide = nn(jnp.concatenate(scores, axis=0), spread).astype(BRAIN)
        prob_wide = nn(jnp.concatenate(probs, axis=0), spread).astype(BRAIN)

        def part(array, f, g):
            return array[(f * frames + g) * size : (f * frames + g + 1) * size]

        keys = [k_in[g, at] for g in range(frames)]
        for f in range(own):
            total = tree_sum(part(score_wide, f, g) * keys[g] for g in range(frames))
            q_out[f, at] = total * jnp.asarray(HEAD_DIM ** (-0.5), BRAIN)
        queries = [q_in[f, at] for f in range(own)]
        for g in range(frames):
            key_grad = tree_sum(part(score_wide, f, g) * queries[f] for f in range(own))
            value_grad = tree_sum(part(prob_wide, f, g) * att[f] for f in range(own))
            if g < own:
                own_out[0, g, at] = key_grad
                own_out[1, g, at] = value_grad
            else:
                far_out[0, g - own, at] = key_grad
                far_out[1, g - own, at] = value_grad
        return carry

    lax.fori_loop(0, rows // size, chunk, 0, unroll=True)


def time_mix_back_kernel(info, tokens, vectors, mixed, after_grad, w_mine, w_other, token_out, sums, held, sems):
    step = pl.program_id(0)
    width = tokens.shape[-1]

    copies = column_copies(info[0], w_mine, w_other, held, sems)
    start_first(copies)

    @pl.when(step == 0)
    def _():
        sums[...] = jnp.zeros_like(sums)

    mixed_grad = merged(mixed)
    sums[2:3] = sums[2:3] + column_sum(mixed_grad[:, :width].astype(FLOAT))
    sums[3:4] = sums[3:4] + column_sum(mixed_grad[:, 2 * width :].astype(FLOAT))
    unit, inverse = unit_of(merged(tokens).astype(FLOAT))
    wait_first(copies)
    upstream = nt(mixed_grad, held[...])
    result = merged(after_grad) + norm_back(unit, inverse, vectors[0:1], upstream)
    token_out[...] = result.reshape(mixed.shape[:2] + (width,))[:, : token_out.shape[1]]
    sums[0:1] = sums[0:1] + column_sum(upstream * unit)
    sums[1:2] = sums[1:2] + column_sum(upstream)


def mixed_grad_kernel(queries, own, far, out):
    width = queries.shape[2]
    out[:, :, :width] = queries[...]
    out[:, :, width : 2 * width] = (own[0].astype(FLOAT) + far[0].astype(FLOAT)).astype(BRAIN)
    out[:, :, 2 * width :] = (own[1].astype(FLOAT) + far[1].astype(FLOAT)).astype(BRAIN)


def sums_kernel(time_sums, space_sums, mlp_sums, bias, out, lines):
    lines[...] = jnp.zeros_like(lines)
    lines[0:4] = time_sums[0:4]
    lines[4:5] = space_sums[5:6]
    lines[5:10] = space_sums[0:5]
    lines[10:13] = mlp_sums[0:3]
    count = bias.shape[1]
    place = lax.broadcasted_iota(jnp.int32, (count, LANES), 1) == row_index((count, LANES)) + 13
    spread = lax.dot_general(
        bias[...], place.astype(FLOAT), (((1,), (0,)), ((), ())), preferred_element_type=FLOAT,
        precision=lax.Precision.HIGHEST,
    )
    out[...] = lines[...].T + spread


def halves_kernel(left, right, left_out, right_out):
    left_out[...] = left[...]
    right_out[...] = right[...]


def share_rows(info, value, mine, other, at=slice(None)):
    value = value.reshape(mine.shape[0], 2, mine.shape[1], value.shape[-1])
    first = info[0] == 0
    mine[:, :, at] = jnp.where(first, value[:, 0], value[:, 1]).astype(BRAIN)
    other[:, :, at] = jnp.where(first, value[:, 1], value[:, 0]).astype(BRAIN)


def time_outer_kernel(info, left, right, sums, mine, other):
    step = pl.program_id(0)
    width = left.shape[1]

    for n in range(3):

        @pl.when(step == n)
        def _():
            share_rows(info, tn(left[...], right[...]), mine, other, slice(n * width, (n + 1) * width))

    @pl.when(step == 0)
    def _():
        share_rows(info, sums[...], mine, other, slice(3 * width, 3 * width + sums.shape[1]))


def space_outer_kernel(info, low, mixed, att, branch, time_att, time_grad, mine, other):
    step = pl.program_id(0)

    @pl.when(step < 3)
    def _():
        share_rows(info, tn(low[...], mixed[...]), mine, other)

    @pl.when(step == 3)
    def _():
        share_rows(info, tn(att[...], branch[...]), mine, other)

    @pl.when(step == 4)
    def _():
        share_rows(info, tn(time_att[...], time_grad[...]), mine, other)


def mlp_outer_kernel(info, low, before, hidden, feed, mine, other, turned, ups, downs, sems):
    step = pl.program_id(0)
    steps = ups.shape[0]
    blocks, cut, width = ups.shape[1:]
    per = downs.shape[2]

    @pl.when(step == 0)
    def _():
        turned[...] = low[...].T

    ups[step] = nn(turned[...], before[...]).astype(BRAIN).reshape(blocks, cut, width)
    value = tn(hidden[...], feed[...]).astype(BRAIN).reshape(per, 2, 2 * cut, width)
    downs[step, 0] = value[:, 0]
    downs[step, 1] = value[:, 1]

    for n in range(steps):
        targets = (mine, other)
        for k, slot in ((0, info[0]), (1, 1 - info[0])):
            up_copy = pltpu.make_async_copy(
                ups.at[n], targets[k].at[:, (n % 2) * cut : (n % 2 + 1) * cut], sems.at[0, n]
            )
            down_copy = pltpu.make_async_copy(
                downs.at[n, slot], targets[k].at[n * per : (n + 1) * per, 2 * cut :], sems.at[1 + k, n]
            )

            @pl.when((step == n) & (slot == n // 2))
            def _():
                up_copy.start()

            @pl.when(step == n)
            def _():
                down_copy.start()

            @pl.when((step == steps - 1) & (slot == n // 2))
            def _():
                up_copy.wait()

            @pl.when(step == steps - 1)
            def _():
                down_copy.wait()


def smem():
    return pl.BlockSpec(memory_space=pltpu.SMEM)


def hbm():
    return pl.BlockSpec(memory_space=pl.ANY)


def whole(shape):
    return pl.BlockSpec(shape, lambda *_: (0,) * len(shape))


def per_frame(shape, first=0, count=1):
    return pl.BlockSpec((count,) + shape[1:], lambda s: (s + first // count,) + (0,) * (len(shape) - 1))


def sds(shape, kind):
    return jax.ShapeDtypeStruct(shape, kind)


def call(kernel, grid, inputs, outputs, scratch=(), micros=2, deps=(), previous=(), prefetch=0):
    count = len(inputs)
    skip = len(previous) + len(deps)

    def inner(*refs):
        kernel(*refs[:count], *refs[count + skip :])

    specs = [spec for spec, _ in inputs[prefetch:]] + [hbm()] * skip
    common = dict(
        name=getattr(kernel, "func", kernel).__name__,
        out_shape=[shape for _, shape in outputs],
        compiler_params=pltpu.CompilerParams(vmem_limit_bytes=VMEM_BYTES),
        input_output_aliases={count + n: n for n in range(len(previous))},
        cost_estimate=pl.CostEstimate(flops=int(micros * RATE), bytes_accessed=1, transcendentals=0),
    )
    places = dict(grid=grid, in_specs=specs, out_specs=[spec for spec, _ in outputs], scratch_shapes=list(scratch))
    if prefetch:
        common["grid_spec"] = pltpu.PrefetchScalarGridSpec(num_scalar_prefetch=prefetch, **places)
    else:
        common.update(places)
    return pl.pallas_call(inner, **common)(*[array for _, array in inputs], *previous, *deps)


def time_outer(slot, left, right, sums, deps=()):
    rows, width = left.shape
    wide = right.shape[1]
    shape = (BLOCKS, width // (2 * BLOCKS), wide + sums.shape[1])
    return call(
        time_outer_kernel, (3,),
        [
            (smem(), slot), (whole(left.shape), left), (pl.BlockSpec((rows, width), lambda s: (0, s)), right),
            (whole(sums.shape), sums),
        ],
        [(whole(shape), sds(shape, BRAIN))] * 2, micros=8, deps=deps,
    )


def space_outer(slot, low, mixed, *others, deps=()):
    rows, width = low.shape
    shape = (BLOCKS, width // (2 * BLOCKS), width)
    moving = pl.BlockSpec((rows, width), lambda s: (0, jnp.minimum(s, 2)))
    return call(
        space_outer_kernel, (5,),
        [(smem(), slot), (whole(low.shape), low), (moving, mixed)] + [(whole(v.shape), v) for v in others],
        [(pl.BlockSpec(shape, lambda s: (0, 0, s)), sds(shape[:2] + (5 * width,), BRAIN))] * 2, micros=12, deps=deps,
    )


def mlp_outer(slot, low, before, hidden, feed, deps=()):
    rows, width = low.shape
    wide = hidden.shape[1]
    cut = width // BLOCKS
    shape = (BLOCKS, 4 * cut, width)
    fixed = pl.BlockSpec((rows, width), lambda s, info: (0, 0))
    moving = pl.BlockSpec((rows, width), lambda s, info: (0, s))
    return call(
        mlp_outer_kernel, (wide // width,),
        [(None, slot), (fixed, low), (moving, before), (moving, hidden), (fixed, feed)],
        [(hbm(), sds(shape, BRAIN))] * 2,
        [
            pltpu.VMEM((width, rows), BRAIN),
            pltpu.VMEM((wide // width, BLOCKS, cut, width), BRAIN),
            pltpu.VMEM((wide // width, 2, BLOCKS * width // wide, 2 * cut, width), BRAIN),
            pltpu.SemaphoreType.DMA((3, wide // width)),
        ],
        micros=21, deps=deps, prefetch=1,
    )


def gate(value, deps):
    return pl.pallas_call(
        lambda source, *refs: None,
        in_specs=[hbm()] * (1 + len(deps)),
        out_specs=hbm(),
        out_shape=sds(value.shape, value.dtype),
        input_output_aliases={0: 0},
    )(value, *deps)


def stack_at_kernel(info, *refs):
    for n, ref in enumerate(refs[:-1]):
        refs[-1][info[2] ^ n] = ref[...]


def stack_kernel(*refs):
    for n, ref in enumerate(refs[:-1]):
        refs[-1][n] = ref[...]


def add_kernel(left, right, out):
    out[...] = left[...] + right[...]


def add_after(left, right, deps):
    inputs = [(whole(left.shape), left), (whole(right.shape), right)]
    return call(add_kernel, (1,), inputs, [(whole(left.shape), sds(left.shape, left.dtype))], deps=deps)[0]


def assemble_kernel(info, o4, rx, ry, ra, rb, out):
    depth = info[2]
    plane = info[3]
    for m in range(4):
        for n in range(4):
            if n < 3:
                value = (o4, rx, ry)[n][m]
            else:
                value = ra[m] if m < 2 else rb[m - 2]
            out[(depth ^ m) * 4 + (plane ^ n)] = value


def pack_kernel(info, time_qkv, space_qkv, space_proj, time_proj, up, time_vec, space_vec, mlp_vec, bias, send, keep):
    width = time_proj.shape[1]
    half = width // 2
    pieces = [time_qkv[:, n * half : (n + 1) * half] for n in range(6)]
    pieces += [space_qkv[:, n * half : (n + 1) * half] for n in range(6)]
    pieces += [space_proj[:, :half], space_proj[:, half:], time_proj[:, :half], time_proj[:, half:]]
    pieces += [up[:, n * half : (n + 1) * half] for n in range(8)]
    first = info[0] == 0
    at = 0
    for begin, count in ((0, 3), (6, 5), (16, 4)):
        for n in range(count):
            low, high = pieces[begin + n], pieces[begin + count + n]
            keep[:, at : at + half] = jnp.where(first, low, high)
            send[:, at : at + half] = jnp.where(first, high, low)
            at += half
    line = 0
    total = jnp.zeros((keep.shape[0], LANES), FLOAT)
    for source in (time_vec, space_vec, mlp_vec, bias):
        count = source.shape[0]
        lane = lax.broadcasted_iota(jnp.int32, (count, LANES), 1)
        chosen = (lane == row_index((count, LANES)) + line).astype(FLOAT)
        total = total + lax.dot_general(
            source[...].astype(FLOAT), chosen, (((0,), (0,)), ((), ())), preferred_element_type=FLOAT
        )
        line += count
    keep[:, at:] = total.astype(BRAIN)
    send[:, at:] = total.astype(BRAIN)


def turn_kernel(source, out):
    out[...] = source[...].astype(FLOAT).T


def join_kernel(info, keep, come, down, time_out, space_out, mlp_out):
    first = info[0] == 0
    width = down.shape[1]
    mine, far = keep[...].astype(FLOAT), come[...].astype(FLOAT)
    both = jnp.concatenate([jnp.where(first, mine, far), jnp.where(first, far, mine)], axis=0).astype(BRAIN)
    cut = both.shape[0]
    end = time_out.shape[1] - LANES
    time_out[:, :end] = both[:, :end]
    time_out[:, end:] = both[:, both.shape[1] - LANES :]
    space_out[...] = both[:, end : end + space_out.shape[1]]
    at = end + space_out.shape[1]
    mlp_out[:cut] = both[:, at : at + width]
    mlp_out[cut : 2 * cut] = both[:, at + width : at + 2 * width]
    mlp_out[2 * cut :] = down[...]


def added(*values):
    return sum(v.astype(FLOAT) for v in values).astype(BRAIN)


def reduce_first_kernel(info, mine, far, to_y, to_x, near_x, near_y, own):
    step = pl.program_id(0)
    plane = info[3]
    own[0] = added(mine[0, plane], far[0, plane])
    near_x[0] = added(mine[0, plane ^ 1], far[0, plane ^ 1])
    near_y[0] = added(mine[0, plane ^ 2], far[0, plane ^ 2])
    diagonal = added(mine[0, plane ^ 3], far[0, plane ^ 3])

    @pl.when(step < 2)
    def _():
        to_y[0] = diagonal

    @pl.when(step >= 2)
    def _():
        to_x[0] = diagonal


def reduce_second_kernel(near_x, near_y, from_y, from_x, out_x, out_y):
    step = pl.program_id(0)

    @pl.when(step < 2)
    def _():
        out_x[0] = added(near_x[0], from_y[0])
        out_y[0] = near_y[0]

    @pl.when(step >= 2)
    def _():
        out_x[0] = near_x[0]
        out_y[0] = added(near_y[0], from_x[0])


def reduce_third_kernel(info, own, from_x, from_y, *outs):
    for m, out in enumerate(outs):
        at = info[2] ^ m
        out[...] = added(own[at], from_x[at], from_y[at])


def final_kernel(first, second, third, fourth, *outs):
    at = 0
    for out in outs:
        part = slice(at, at + out.shape[1])
        out[...] = (first[:, part].astype(FLOAT) + second[:, part].astype(FLOAT)) + (
            third[:, part].astype(FLOAT) + fourth[:, part].astype(FLOAT)
        )
        at += out.shape[1]


def final_mlp_kernel(first, second, third, fourth, up, down):
    cut, width = up.shape[0], down.shape[1]
    total = (first[...].astype(FLOAT) + second[...].astype(FLOAT)) + (
        third[...].astype(FLOAT) + fourth[...].astype(FLOAT)
    )
    up[:, :width] = total[:cut]
    up[:, width:] = total[cut : 2 * cut]
    down[...] = total[2 * cut :]


def exact(left, right, sides):
    return lax.dot_general(
        left, right, ((sides[:1], sides[1:]), ((), ())), preferred_element_type=FLOAT, precision=lax.Precision.HIGHEST
    )


def final_time_kernel(first, second, third, fourth, out, time_vec, space_vec, mlp_vec, bias):
    total = (first[...].astype(FLOAT) + second[...].astype(FLOAT)) + (
        third[...].astype(FLOAT) + fourth[...].astype(FLOAT)
    )
    end = out.shape[1]
    out[...] = total[:, :end]
    sums = total[:, end:]
    rows = sums.shape[0]
    same = row_index((rows, rows)) == lax.broadcasted_iota(jnp.int32, (rows, rows), 1)
    lines = exact(sums, same.astype(FLOAT), (0, 0))
    at = 0
    for ref in (time_vec, space_vec, mlp_vec):
        ref[...] = lines[at : at + ref.shape[0]]
        at += ref.shape[0]
    count = bias.shape[1]
    chosen = row_index((LANES, count)) == lax.broadcasted_iota(jnp.int32, (LANES, count), 1) + at
    bias[...] = exact(sums, chosen.astype(FLOAT), (1, 0))


def reduce_fourth_kernel(first, second, come, first_out, second_out):
    first_out[...] = first[...].astype(FLOAT) + come[0].astype(FLOAT)
    second_out[...] = added(second[...], come[1])


def clip_swap(values, bits, count):
    return lax.ppermute(values, "clip", [(i, i ^ bits) for i in range(count)])


def core_swap(values):
    return lax.ppermute(values, "frame", [(0, 1), (1, 0)])


class Near:
    def __init__(self, clips, info):
        self.clips = clips
        self.info = info
        self.core = lax.axis_index("frame")

    def swap(self, values, bits):
        return clip_swap(values, bits, self.clips)

    def in_order(self, mine, far, axis):
        return jnp.where(
            self.core == 0, jnp.concatenate([mine, far], axis=axis), jnp.concatenate([far, mine], axis=axis)
        )

    def stack(self, pieces, deps):
        shape = (len(pieces),) + pieces[0].shape
        return call(
            stack_kernel, (1,), [(whole(v.shape), v) for v in pieces], [(whole(shape), sds(shape, BRAIN))],
            micros=3, deps=deps,
        )[0]

    def depth_direct(self, own, deps):
        return self.stack([own] + [self.swap(own, 4 * m) for m in (1, 2, 3)], deps)

    def depth_in_order(self, own, deps):
        pieces = [own] + [self.swap(own, 4 * m) for m in (1, 2, 3)]
        shape = (4,) + own.shape
        return call(
            stack_at_kernel, (1,), [(smem(), self.info)] + [(whole(v.shape), v) for v in pieces],
            [(whole(shape), sds(shape, BRAIN))], micros=3, deps=deps,
        )[0]

    def depth_near(self, own, deps):
        return self.stack([own, self.swap(own, 4)], deps)

    def depth_far(self, two, deps):
        come = self.swap(two, 8)
        return self.stack([two[0], two[1], come[0], come[1]], deps)

    def plane_step(self, o4, deps):
        rx = self.swap(o4, 1)
        ry = self.swap(o4, 2)
        half = (2,) + o4.shape[1:]
        first = pl.BlockSpec(half, lambda s: (0, 0, 0))
        second = pl.BlockSpec(half, lambda s: (1, 0, 0))
        sx, sy = call(
            halves_kernel, (1,), [(first, rx), (second, ry)], [(whole(half), sds(half, BRAIN))] * 2, deps=deps
        )
        return rx, ry, sx, sy

    def diagonal_step(self, o4, planes, deps):
        rx, ry, sx, sy = planes
        pieces = (o4, rx, ry, self.swap(sx, 2), self.swap(sy, 1))
        shape = (self.clips,) + o4.shape[1:]
        return call(
            assemble_kernel, (1,), [(smem(), self.info)] + [(whole(v.shape), v) for v in pieces],
            [(whole(shape), sds(shape, BRAIN))], micros=3, deps=deps,
        )[0]

    def reduce_first(self, mine, far, deps, micros=20):
        block = mine.shape[1:]
        four = (4, 4) + block
        view = pl.BlockSpec((1, 4) + block, lambda s: (s, 0, 0, 0))
        one = lambda pick: pl.BlockSpec((1,) + block, lambda s: (pick(s), 0, 0))
        each = (one(lambda s: s), sds((4,) + block, BRAIN))
        return call(
            reduce_first_kernel, (4,),
            [(smem(), self.info), (view, mine.reshape(four)), (view, far.reshape(four))],
            [
                (one(lambda s: jnp.minimum(s, 1)), sds((2,) + block, BRAIN)),
                (one(lambda s: jnp.maximum(s - 2, 0)), sds((2,) + block, BRAIN)),
                each, each, each,
            ],
            micros=micros, deps=deps,
        )

    def reduce_second(self, near_x, near_y, to_y, to_x, deps):
        from_y, from_x = self.swap(to_y, 2), self.swap(to_x, 1)
        block = near_x.shape[1:]
        one = lambda pick: pl.BlockSpec((1,) + block, lambda s: (pick(s), 0, 0))
        each = one(lambda s: s)
        return call(
            reduce_second_kernel, (4,),
            [
                (each, near_x), (each, near_y), (one(lambda s: jnp.minimum(s, 1)), from_y),
                (one(lambda s: jnp.maximum(s - 2, 0)), from_x),
            ],
            [(each, sds(near_x.shape, BRAIN))] * 2, micros=20, deps=deps,
        )

    def reduce_third(self, own, near_x, near_y, deps):
        from_x, from_y = self.swap(near_x, 1), self.swap(near_y, 2)
        block = own.shape[1:]
        return call(
            reduce_third_kernel, (1,),
            [(smem(), self.info)] + [(whole(v.shape), v) for v in (own, from_x, from_y)],
            [(whole(block), sds(block, BRAIN))] * 4,
            micros=20, deps=deps,
        )

    def reduce_fourth(self, first, second, others, deps):
        come = self.swap(others, 8)
        inputs = [(whole(v.shape), v) for v in (first, second, come)]
        outs = [(whole(first.shape), sds(first.shape, kind)) for kind in (FLOAT, BRAIN)]
        return call(reduce_fourth_kernel, (1,), inputs, outs, micros=20, deps=deps)

    def reduce_end(self, first, second):
        return first + self.swap(second, 4).astype(FLOAT)

    def reduce_direct(self, first, second, third, fourth, shapes, kernel=final_kernel, deps=()):
        pieces = [first, self.swap(second, 4), self.swap(third, 8), self.swap(fourth, 12)]
        inputs = [(whole(v.shape), v) for v in pieces]
        return call(kernel, (1,), inputs, [(whole(n), sds(n, FLOAT)) for n in shapes], deps=deps)

    def owner_rows(self, value):
        rows = value.shape[0] // 2
        mine = lax.dynamic_slice_in_dim(value, self.core * rows, rows, 0)
        theirs = lax.dynamic_slice_in_dim(value, (1 - self.core) * rows, rows, 0)
        return self.in_order(mine, core_swap(theirs), 1)


AXES = ("clip", "frame")


def body(
    clips, cores, clip_tokens, clip_class, output_grad, class_grad, clip_count,
    time_qkv, time_proj, time_vec, space_qkv, space_proj, space_vec, mlp_up, mlp_down, mlp_vec, mlp_bias,
):
    _, own, places_here, width = clip_tokens.shape
    rows = -(-(places_here + 1) // 16) * 16
    frames = own * cores
    wide = mlp_up.shape[1]
    cut = width // BLOCKS
    core = lax.axis_index("frame")
    place = lax.axis_index("clip")
    shard = place * cores + core
    leader = (core == 0).astype(jnp.int32)
    alive = (jnp.arange(1, dtype=jnp.int32) < clip_count[0]).astype(FLOAT)
    is_near = clips == 16 and cores == 2
    slot = core if is_near else core * 0
    info = jnp.stack([slot, leader, place // 4, place % 4, shard]).astype(jnp.int32)
    near = Near(clips, info) if is_near else None
    my_slot = info[0:1]
    far_slot = 1 - my_slot

    class_block = jnp.broadcast_to(clip_class[0][None, None], (own, 1, width))
    blank = jnp.zeros((own, rows - places_here - 1, width), BRAIN)
    tokens = jnp.concatenate([clip_tokens[0], class_block, blank], axis=1)
    last = (jnp.arange(own) == own - 1)[:, None, None]
    class_rows = jnp.where(last, class_grad[0][None, None], jnp.zeros((), BRAIN))
    grads = jnp.concatenate([output_grad[0], class_rows, blank], axis=1)

    bias_rows = wide // width
    zeros = jnp.zeros((8, width), FLOAT)
    flat = lambda v: v.reshape((own * rows,) + v.shape[2:])

    if near is not None:
        packed = (
            time_qkv, space_qkv, space_proj, time_proj, mlp_up, time_vec, space_vec, mlp_vec,
            mlp_bias.reshape(-1, bias_rows).T,
        )
        line = sds((time_qkv.shape[0], 6 * width + LANES), BRAIN)
        send, keep = call(
            pack_kernel, (1,), [(smem(), info)] + [(whole(v.shape), v) for v in packed],
            [(whole(line.shape), line), (whole(line.shape), line)],
        )
        shapes = [(cut, 3 * width // 2 + LANES), (cut, 5 * width // 2), (4 * cut, width)]
        time_own, space_own, mlp_own = call(
            join_kernel, (1,),
            [(smem(), info)] + [(whole(v.shape), v) for v in (keep, core_swap(send), mlp_down)],
            [(whole(shape), sds(shape, BRAIN)) for shape in shapes],
        )
        join = lambda two: tuple(h.reshape(width, h.shape[-1]) for h in two)
        time_line = near.depth_direct(time_own, [])
        far_tokens = core_swap(gate(tokens, [time_own]))
        space_own = gate(space_own, [time_line])
        space_line = near.depth_direct(space_own, [])
        time_mine = near.diagonal_step(time_line, near.plane_step(time_line, []), [grads, far_tokens, space_line])
        space_line = gate(space_line, [time_mine])
        time_far = core_swap(time_mine)
        time_w = join((time_mine, time_far))
        vec_block = pl.BlockSpec((width, LANES), lambda s: (0, time_w[0].shape[1] // LANES - 1))
        vectors = call(
            turn_kernel, (1,), [(vec_block, time_w[0])], [(whole((LANES, width)), sds((LANES, width), FLOAT))],
            deps=[space_line],
        )[0]
        n_vec = time_vec.shape[0] + space_vec.shape[0] + mlp_vec.shape[0]
        bias = vectors[n_vec : n_vec + bias_rows].T.reshape(bias_rows, width)
        mlp_own = gate(mlp_own, [time_mine])
        mix_deps = [space_line, mlp_own]
    else:
        everywhere = lax.all_gather(tokens, "frame", axis=0, tiled=True)
        far_tokens = jnp.roll(everywhere, -core * own, axis=0)[own:]
        vec_shard = jnp.concatenate([time_vec, space_vec, mlp_vec], axis=0)
        blank_rows = jnp.zeros((16 - vec_shard.shape[0], width), FLOAT)
        space_shard = jnp.concatenate([space_qkv, space_proj, time_proj], axis=1)
        vectors = lax.all_gather(vec_shard, AXES, axis=1, tiled=True).astype(FLOAT)
        bias = lax.all_gather(mlp_bias, AXES, axis=0, tiled=True).astype(FLOAT).reshape(bias_rows, width)
        vectors = jnp.concatenate([vectors, blank_rows], axis=0)

        def halves(value):
            full = lax.all_gather(value, AXES, axis=0, tiled=True)
            half = full.shape[1] // 2
            return full[:, :half], full[:, half:]

        time_w, space_w = halves(time_qkv), halves(space_shard)
        up = lax.all_gather(mlp_up, AXES, axis=0, tiled=True).reshape(BLOCKS, cut, 2, 2, width)
        up = jnp.transpose(up, (2, 0, 3, 1, 4)).reshape(2, BLOCKS, 2 * cut, width)
        down = lax.all_gather(mlp_down, AXES, axis=0, tiled=True).reshape(BLOCKS, 2, 2 * cut, width)
        mlp_w = tuple(
            (jnp.concatenate([up[n], down[:, n]], axis=1).reshape(4, BLOCKS // 4, 4 * cut, width),) for n in (0, 1)
        )
        mix_deps = []

    frame_shape = (own, rows, width)
    out_shape = (own, places_here, width)
    all_shape = (frames, rows, width)
    heads = width // HEAD_DIM
    prob_shape = (own, frames, rows, LANES)
    sprob_shape = (own, heads, rows, rows)
    mixed_shape = (own, rows, 3 * width)
    hidden_shape = (own, rows, wide)
    sum_out = (whole((8, width)), sds((8, width), FLOAT))
    row_bytes = own * rows * width
    square = 2 * own * rows * width * width
    group = 2 if own % 2 == 0 else 1
    frames_in = lambda array, first=0: (per_frame(array.shape, first, group), array)
    low_out = lambda shape, first=0: (per_frame(shape, first, group), sds(shape, BRAIN))
    wide_out = lambda shape, first=0: (per_frame(shape, first, group), sds(shape, FLOAT))
    vec_in = (whole(vectors.shape), vectors)
    pair = lambda two: [(hbm(), two[0]), (hbm(), two[1])]
    time_held = [pltpu.VMEM((width, 3 * width), BRAIN), pltpu.SemaphoreType.DMA((2,))]
    space_held = [pltpu.VMEM((width, 5 * width), BRAIN), pltpu.SemaphoreType.DMA((2,))]
    mlp_held = [
        pltpu.VMEM((wide // width, 4, BLOCKS // 4, cut, width), BRAIN),
        pltpu.VMEM((4, BLOCKS // 4, 2, 2 * cut, width), BRAIN),
        pltpu.SemaphoreType.DMA((2, 15)),
    ]

    own_map = pl.BlockSpec((group, rows, width), lambda s: (jnp.minimum(s, own // group - 1), 0, 0))
    far_map = pl.BlockSpec((group, rows, width), lambda s: (jnp.maximum(s - own // group, 0), 0, 0))
    queries, key_rows, value_rows, time_low = call(
        functools.partial(time_mix_kernel, own // group), (frames // group,),
        [(smem(), info), (own_map, tokens), (far_map, far_tokens), vec_in] + pair(time_w),
        [(own_map, sds(frame_shape, BRAIN)), low_out(all_shape), low_out(all_shape), (own_map, sds(frame_shape, BRAIN))],
        time_held, micros=1, deps=mix_deps,
    )

    if near is not None:
        mlp_line = near.depth_in_order(mlp_own, [queries])
        space_mine = near.diagonal_step(space_line, near.plane_step(space_line, [queries]), [mlp_line])
        space_w = join((space_mine, core_swap(space_mine)))
        mlp_line = gate(mlp_line, [space_mine])

    parts = [(0, own)]
    deps = [] if near is None else [mlp_line]
    kept, class_own = (), zeros
    for first, count in parts:
        outs = call(
            functools.partial(attention_kernel, places_here), (count // group,),
            [
                (smem(), info), frames_in(tokens, first), vec_in, frames_in(queries, first),
                (whole(all_shape), key_rows), (whole(all_shape), value_rows), (whole((8, width)), class_own),
            ]
            + pair(space_w),
            [
                low_out(prob_shape, first), low_out(frame_shape, first), wide_out(frame_shape, first),
                low_out(frame_shape, first), low_out(mixed_shape, first), low_out(sprob_shape, first),
                low_out(frame_shape, first), wide_out(frame_shape, first), sum_out,
            ],
            space_held, micros=27 * count / own, deps=deps, previous=kept,
        )
        kept, class_own = tuple(outs[:-1]), outs[-1]
        if near is not None and first == 0:
            mlp_planes = near.plane_step(mlp_line, [class_own])
            deps = list(mlp_planes[2:])
    time_prob, time_att, after, space_low, space_mixed, space_prob, space_att, places = kept

    if near is not None:
        rx, ry, sx, sy = mlp_planes
        mlp_first = tuple(gate(v, [sx, sy]) for v in (mlp_line, rx, ry))
        mlp_last = (near.swap(sx, 2), near.swap(sy, 1))
        mlp_w = (mlp_first + mlp_last, tuple(core_swap(v) for v in mlp_first) + tuple(core_swap(v) for v in mlp_last))
        class_far = core_swap(class_own)
    else:
        class_far = lax.psum(class_own, "frame") - class_own
    class_row = jnp.broadcast_to(clip_class.astype(FLOAT), (8, width))
    small = whole((8, width))
    result, class_result, mlp_low, hidden, feed_grad, before_grad, rows_grad, mlp_sums = call(
        functools.partial(mlp_kernel, places_here, frames, len(mlp_w[0])), (own // group,),
        [
            (smem(), info), (smem(), alive), frames_in(places), frames_in(grads),
            (small, class_row), (small, class_own), (small, class_far), vec_in, (whole(bias.shape), bias),
        ]
        + [(hbm(), v) for v in mlp_w[0] + mlp_w[1]],
        [
            low_out(out_shape), sum_out, low_out(frame_shape), low_out(hidden_shape), low_out(frame_shape),
            low_out(hidden_shape), wide_out(frame_shape), sum_out,
        ],
        [pltpu.VMEM((wide // width, group * rows, width), FLOAT)] + mlp_held,
        micros=25,
    )

    mlp_mine, mlp_far = mlp_outer(my_slot, flat(mlp_low), flat(before_grad), flat(hidden), flat(feed_grad))
    class_block_at = places_here // 16
    class_spec = pl.BlockSpec((1, 16, width), lambda s: (own - 1, class_block_at, 0))

    def space_back(first, count, sums, deps, previous):
        return call(
            functools.partial(space_back_kernel, places_here, frames), (count // group,),
            [
                (smem(), info), frames_in(rows_grad, first), (class_spec, rows_grad), frames_in(after, first),
                frames_in(space_mixed, first), frames_in(space_prob, first), frames_in(space_att, first),
                vec_in, (small, sums),
            ]
            + pair(space_w),
            [
                low_out(frame_shape, first), low_out(mixed_shape, first), wide_out(frame_shape, first),
                low_out(frame_shape, first), low_out(frame_shape, first), sum_out,
            ],
            space_held, micros=30 * count / own, deps=deps, previous=previous,
        )

    half = own // 2
    if near is not None:
        outs = space_back(0, half, zeros, [mlp_far], ())
        mlp_a, mlp_b, mlp_x, mlp_y, mlp_own = near.reduce_first(mlp_mine, core_swap(mlp_far), [outs[0]])
        outs = space_back(half, own - half, outs[-1], [mlp_a, mlp_b], tuple(outs[:-1]))
        mlp_x, mlp_y = near.reduce_second(mlp_x, mlp_y, mlp_a, mlp_b, [outs[0]])
        time_deps = [mlp_x, mlp_y]
    else:
        outs = space_back(0, own, zeros, [], ())
        time_deps = []
    branch_grad, space_mixed_grad, after_grad, time_grad, time_att_grad, space_sums = outs

    space_mine, space_far = space_outer(
        my_slot, *[flat(v) for v in (space_low, space_mixed_grad, space_att, branch_grad, time_att, time_grad)],
        deps=time_deps,
    )
    time_deps = time_deps + [space_far]
    far_frames = frames - own
    lanes_of = lambda shape: pl.BlockSpec(shape[:-1] + (2 * LANES,), lambda s: (0,) * (len(shape) - 1) + (s,))
    lanes_in = lambda v: (lanes_of(v.shape), v)
    q_grad, own_grad, far_grad = call(
        time_back_kernel, (width // LANES // 2,),
        [
            lanes_in(queries), lanes_in(key_rows), lanes_in(value_rows), (whole(prob_shape), time_prob),
            lanes_in(time_att_grad),
        ],
        [
            (lanes_of(shape), sds(shape, BRAIN))
            for shape in (frame_shape, (2,) + frame_shape, (2, far_frames, rows, width))
        ],
        micros=19, deps=time_deps,
    )
    if near is not None:
        from_far = core_swap(far_grad)
        mlp_first, mlp_second, *mlp_others = near.reduce_third(mlp_own, mlp_x, mlp_y, [q_grad])
        space_a, space_b, space_x, space_y, space_own = near.reduce_first(space_mine, core_swap(space_far), [mlp_second])
        mixed_deps = [space_own]
    else:
        mixed_deps = []
        padded = jnp.concatenate([jnp.zeros_like(own_grad), far_grad], axis=1)
        padded = jnp.roll(padded, core * own, axis=1)
        from_far = lax.psum_scatter(padded, "frame", scatter_dimension=1, tiled=True)
    pair_in = lambda v: (pl.BlockSpec((2, group, rows, width), lambda s: (0, s, 0, 0)), v)
    time_mixed_grad = call(
        mixed_grad_kernel, (own // group,), [frames_in(q_grad), pair_in(own_grad), pair_in(from_far)],
        [low_out(mixed_shape)], micros=3, deps=mixed_deps,
    )[0]
    outer = (flat(time_low), flat(time_mixed_grad))

    back_deps = []
    if near is not None:
        space_x, space_y = near.reduce_second(space_x, space_y, space_a, space_b, [time_mixed_grad])
        back_deps = [mlp_second, space_x, space_y]
    token_grad, time_sums = call(
        time_mix_back_kernel, (own // group,),
        [(smem(), info), frames_in(tokens), vec_in, frames_in(time_mixed_grad), frames_in(after_grad)]
        + pair(time_w),
        [wide_out(out_shape), sum_out],
        time_held, micros=4, deps=back_deps,
    )
    bias_grad = mlp_sums[3 : 3 + bias_rows].reshape(width, bias_rows)
    n_sums = 13
    sums = call(
        sums_kernel, (1,), [(small, time_sums), (small, space_sums), (small, mlp_sums), (whole(bias_grad.shape), bias_grad)],
        [(whole((width, LANES)), sds((width, LANES), FLOAT))], [pltpu.VMEM((LANES, width), FLOAT)],
    )[0]

    if near is not None:
        up_rows, grad_mlp_down = near.reduce_direct(
            mlp_first, mlp_second, *mlp_others, [(cut, 2 * width), (2 * cut, width)], final_mlp_kernel, [token_grad]
        )
        space_parts = near.reduce_third(space_own, space_x, space_y, [up_rows])
        time_mine, time_far = time_outer(my_slot, *outer, sums, deps=[space_parts[1]])
        time_a, time_b, time_x, time_y, time_own = near.reduce_first(time_mine, core_swap(time_far), [])
        time_x, time_y = near.reduce_second(time_x, time_y, time_a, time_b, [])
        time_parts = near.reduce_third(time_own, time_x, time_y, [])
        half = cut // 2
        space_grads = near.reduce_direct(*space_parts, [(half, 3 * width), (half, width), (half, width)])
        vec_shapes = [(v.shape[0], half) for v in (time_vec, space_vec, mlp_vec)]
        grad_time, grad_time_vec, grad_space_vec, grad_mlp_vec, bias_rows_grad = near.reduce_direct(
            *time_parts, [(half, 3 * width)] + vec_shapes + [(half, bias_rows)], final_time_kernel
        )
        grad_mlp_bias = bias_rows_grad.reshape(-1)
        grad_mlp_up = near.owner_rows(up_rows)
        class_total = space_sums[6:7] + core_swap(space_sums)[6:7]
    else:
        send = lambda v: lax.psum_scatter(v, AXES, scatter_dimension=0, tiled=True).astype(FLOAT)
        spread = lambda mine, far: jnp.stack([mine, far], axis=1).reshape(width, mine.shape[2])
        time_mine, time_far = time_outer(my_slot, *outer, sums)
        up = jnp.stack([v[:, : 2 * cut].reshape(BLOCKS, 2, cut, width) for v in (mlp_mine, mlp_far)])
        grad_mlp_up = send(jnp.transpose(up, (1, 3, 0, 2, 4)).reshape(width, wide))
        grad_mlp_down = send(jnp.stack([v[:, 2 * cut :] for v in (mlp_mine, mlp_far)], axis=1).reshape(wide, width))
        grad_space = send(spread(space_mine, space_far))
        space_grads = (grad_space[:, : 3 * width], grad_space[:, 3 * width : 4 * width], grad_space[:, 4 * width :])
        grad_time = send(spread(time_mine, time_far)[:, : 3 * width])
        class_total = lax.psum(space_sums[6:7], "frame")
        step = width // (clips * cores)
        sums = lax.dynamic_slice_in_dim(lax.psum(sums, AXES), shard * step, step, 0)
        lines = sums.T
        grad_time_vec, grad_space_vec, grad_mlp_vec = lines[:5], lines[5:10], lines[10:13]
        grad_mlp_bias = sums[:, n_sums : n_sums + bias_rows].reshape(-1)
    class_in_grad = rows_grad[own - 1, places_here][None] + class_total
    return (
        result[None],
        class_result[places_here % 8][None].astype(BRAIN),
        token_grad[None],
        class_in_grad,
        grad_time,
        space_grads[2],
        grad_time_vec,
        space_grads[0],
        space_grads[1],
        grad_space_vec,
        grad_mlp_up,
        grad_mlp_down,
        grad_mlp_vec,
        grad_mlp_bias,
    )


def solution(mesh):
    both = ("clip", "frame")
    rows = P(both, None)
    columns = P(None, both)
    weights = (rows, rows, columns, rows, rows, columns, rows, rows, columns, P(both))
    block = P("clip", "frame", None, None)
    classes = P("clip", None)
    return jax.shard_map(
        functools.partial(body, mesh.shape["clip"], mesh.shape["frame"]),
        mesh=mesh,
        in_specs=(block, classes, block, classes, P("clip")) + weights,
        out_specs=(block, classes, block, classes) + weights,
        check_vma=False,
    )
```

profile of v0, /device:TPU:0, one launch (start us, length us, event | category | flops | bytes accessed | tf_op | source)
XLA Modules:
  0.0 391.5 jit_solution(4189999475358091193)
XLA Ops:
  20.8 5.3 %collective-permute-done.2.refs_2_ = bf16[48,1280]{1,0:T(8,128)(2,1)S(1)} collective-permute-done((bf16[48,1280]{1,0:T(8,128)(2,1)}, bf16[48,1280]{1,0:T(8,128)(2,1)S(1)}, u32[]{:S(2)}, u32[]{:S(2)}) %collective-permute-start.2) | collective-permute-done | bytes 122912 | tf_op jit(solution)/shard_map/ppermute | solution.py:808
  36.0 4.3 %collective-permute-done.4.refs_0_.refs_2_ = bf16[4,48,1280]{2,1,0:T(8,128)(2,1)S(1)} collective-permute-done((bf16[4,48,1280]{2,1,0:T(8,128)(2,1)}, bf16[4,48,1280]{2,1,0:T(8,128)(2,1)S(1)}, u32[]{:S(2)}, u32[]{:S(2)}) %collective-permute-start.4) | collective-permute-done | bytes 491552 | tf_op jit(solution)/shard_map/ppermute | solution.py:808
  66.3 13.0 %time_mix_kernel.1 = (bf16[4,208,768]{2,1,0:T(8,128)(2,1)}, bf16[8,208,768]{2,1,0:T(8,128)(2,1)}, bf16[8,208,768]{2,1,0:T(8,128)(2,1)}, bf16[4,208,768]{2,1,0:T(8,128)(2,1)}) custom-call(s32[5]{0:T(128)} %stack.27.refs_0_, bf16[4,208,768]{2,1,0:T(8,128)(2,1)} %copy-done, bf16[4,208,768]{2,1,0:T(8,128)(2,1)} %copy-done.5, ...), custom_call_target="tpu_custom_call" | custom-call | flops 1000000000 | bytes 1 | tf_op jit(solution)/shard_map/time_mix_kernel/pallas_call | solution.py:577
  87.6 4.5 %collective-permute-done.15.refs_4_ = bf16[2,48,1920]{2,1,0:T(8,128)(2,1)S(1)} collective-permute-done((bf16[2,48,1920]{2,1,0:T(8,128)(2,1)}, bf16[2,48,1920]{2,1,0:T(8,128)(2,1)S(1)}, u32[]{:S(2)}, u32[]{:S(2)}) %collective-permute-start.15) | collective-permute-done | bytes 368672 | tf_op jit(solution)/shard_map/ppermute | solution.py:808
  99.3 4.0 %collective-permute-done.20 = bf16[16,48,1920]{2,1,0:T(8,128)(2,1)} collective-permute-done((bf16[16,48,1920]{2,1,0:T(8,128)(2,1)}, bf16[16,48,1920]{2,1,0:T(8,128)(2,1)}, u32[]{:S(2)}, u32[]{:S(2)}) %collective-permute-start.20) | collective-permute-done | bytes 2949152 | tf_op jit(solution)/shard_map/ppermute | solution.py:812
  103.9 24.8 %attention_kernel.1 = (bf16[4,8,208,128]{3,2,1,0:T(8,128)(2,1)}, bf16[4,208,768]{2,1,0:T(8,128)(2,1)}, f32[4,208,768]{2,1,0:T(8,128)}, bf16[4,208,768]{2,1,0:T(8...) custom-call(s32[5]{0:T(128)} %stack.27.refs_0_, ...), custom_call_target="tpu_custom_call" | custom-call | flops 27000000512 | bytes 1 | tf_op jit(solution)/shard_map/attention_kernel/pallas_call | solution.py:577
  136.5 12.8 %collective-permute-done.24.refs_12_ = bf16[2,192,768]{2,1,0:T(8,128)(2,1)} collective-permute-done((bf16[2,192,768]{2,1,0:T(8,128)(2,1)}, bf16[2,192,768]{2,1,0:T(8,128)(2,1)}, u32[]{:S(2)}, u32[]{:S(2)}) %collective-permute-start.24) | collective-permute-done | bytes 589856 | tf_op jit(solution)/shard_map/ppermute | solution.py:808
  155.2 25.7 %mlp_kernel.1 = (bf16[4,196,768]{2,1,0:T(8,128)(2,1)}, f32[8,768]{1,0:T(8,128)}, bf16[4,208,768]{2,1,0:T(8,128)(2,1)}, bf16[4,208,3072]{2,1,0:T(8,128)(2,1)}, bf...) custom-call(s32[5]{0:T(128)} %stack.27.refs_0_, ...), custom_call_target="tpu_custom_call" | custom-call | flops 24999999488 | bytes 1 | tf_op jit(solution)/shard_map/mlp_kernel/pallas_call | solution.py:577
  180.9 16.1 %mlp_outer_kernel.1 = (bf16[16,192,768]{2,1,0:T(8,128)(2,1)}, bf16[16,192,768]{2,1,0:T(8,128)(2,1)}) custom-call(s32[1]{0:T(128)} %bitcast.refs_0_, bf16[832,768]{1,0:T(8,128)(2,1)} %bitcast.63, bf16[832,3072]{1,0:T(8,128)(2,1)} %bitcast.52, bf16[832,3072]{1,0:T(8,128)(2,1)} %bitcast.51, bf16[832,768]{1,0:T(8,128)(2,1)} %bitcast.64), custom_call_target="tpu_custom_call" | custom-call | flops 20999999488 | bytes 1 | tf_op jit(solution)/shard_map/mlp_outer_kernel/pallas_call | solution.py:577
  197.6 16.2 %space_back_kernel.2 = (bf16[4,208,768]{2,1,0:T(8,128)(2,1)}, bf16[4,208,2304]{2,1,0:T(8,128)(2,1)}, f32[4,208,768]{2,1,0:T(8,128)}, bf16[4,208,768]{2,1,0:T(8,1...) custom-call(s32[5]{0:T(128)} %stack.27.refs_0_, f32[4,208,768]{2,1,0:T(8,128)} %get-tuple-element.131.refs_1_.refs_2_, ...), custom_call_target="tpu_custom_call" | custom-call | flops 15000000512 | bytes 1 | tf_op jit(solution)/shard_map/space_back_kernel/pallas_call | solution.py:577
  213.9 6.8 %reduce_first_kernel.3 = (bf16[2,192,768]{2,1,0:T(8,128)(2,1)}, bf16[2,192,768]{2,1,0:T(8,128)(2,1)}, bf16[4,192,768]{2,1,0:T(8,128)(2,1)}, bf16[4,192,768]{2,1,0:T(8,128)(2,1)}, bf16[4,192,768]{2,1,0:T(8,128)(2,1)}) custom-call(s32[5]{0:T(128)} %stack.27.refs_0_, bf16[4,4,192,768]{3,2,1,0:T(8,128)(2,1)} %bitcast.53, ...), custom_call_target="tpu_custom_call" | custom-call | flops 20000000000 | bytes 1 | tf_op jit(solution)/shard_map/reduce_first_kernel/pallas_call | solution.py:577
  222.4 16.3 %space_back_kernel.3 = (bf16[4,208,768]{2,1,0:T(8,128)(2,1)}, bf16[4,208,2304]{2,1,0:T(8,128)(2,1)}, f32[4,208,768]{2,1,0:T(8,128)}, bf16[4,208,768]{2,1,0:T(8,1...) custom-call(s32[5]{0:T(128)} %stack.27.refs_0_, ...), custom_call_target="tpu_custom_call", output_to_operand_aliasing={{0}: (11, {}), {1}: (12, {}), {2}: (13, {}), {3}: (14, {}),... | custom-call | flops 15000000512 | bytes 1 | tf_op jit(solution)/shard_map/space_back_kernel/pallas_call | solution.py:577
  239.7 4.3 %reduce_second_kernel.3 = (bf16[4,192,768]{2,1,0:T(8,128)(2,1)}, bf16[4,192,768]{2,1,0:T(8,128)(2,1)}) custom-call(bf16[4,192,768]{2,1,0:T(8,128)(2,1)} %get-tuple-element.151.refs_0_, bf16[4,192,768]{2,1,0:T(8,128)(2,1)} %get-tuple-element.152.refs_1_, bf16[2,192,768]{2,1,0:T(8,128)(2,1)} %copy-done.21, bf16[2,192,768]{2,1,0:T(8,128)(2,1)} %copy-done.22, ...), custom_call_target="tpu_custom_call" | custom-call | flops 20000000000 | bytes 1 | tf_op jit(solution)/shard_map/reduce_second_kernel/pallas_call | solution.py:577
  246.4 12.0 %space_outer_kernel.1 = (bf16[16,24,3840]{2,1,0:T(8,128)(2,1)}, bf16[16,24,3840]{2,1,0:T(8,128)(2,1)}) custom-call(s32[1]{0:T(128)} %bitcast.refs_0_, bf16[832,768]{1,0:T(8,128)(2,1)} %bitcast.59, bf16[832,2304]{1,0:T(8,128)(2,1)} %bitcast.55, bf16[832,768]{1,0:T(8,128)(2,1)} %bitcast.60, bf16[832,768]{1,0:T(8,128)(2,1)} %bitcast.61, ...), custom_call_target="tpu_custom_call" | custom-call | flops 12000000000 | bytes 1 | tf_op jit(solution)/shard_map/space_outer_kernel/pallas_call | solution.py:577
  258.3 16.1 %time_back_kernel.1 = (bf16[4,208,768]{2,1,0:T(8,128)(2,1)}, bf16[2,4,208,768]{3,2,1,0:T(8,128)(2,1)}, bf16[2,4,208,768]{3,2,1,0:T(8,128)(2,1)}) custom-call(bf16[4,208,768]{2,1,0:T(8,128)(2,1)} %get-tuple-element.119.refs_2_.refs_5_.refs_3_.refs_0_, bf16[8,208,768]{2,1,0:T(8,128)(2,1)} %get-tuple-element.120.refs_4_.refs_1_, ...), custom_call_target="tpu_custom_call" | custom-call | flops 19000000512 | bytes 1 | tf_op jit(solution)/shard_map/time_back_kernel/pallas_call | solution.py:577
  279.8 5.1 %reduce_first_kernel.4 = (bf16[2,24,3840]{2,1,0:T(8,128)(2,1)}, bf16[2,24,3840]{2,1,0:T(8,128)(2,1)}, bf16[4,24,3840]{2,1,0:T(8,128)(2,1)}, bf16[4,24,3840]{2,1,0:T(8,128)(2,1)}, bf16[4,24,3840]{2,1,0:T(8,128)(2,1)}) custom-call(s32[5]{0:T(128)} %stack.27.refs_0_, bf16[4,4,24,3840]{3,2,1,0:T(8,128)(2,1)} %bitcast.56, bf16[4,4,24,3840]{3,2,1,0:T(8,128)(2,1)} %bitcast.49, ...), custom_call_target="tpu_custom_call" | custom-call | flops 20000000000 | bytes 1 | tf_op jit(solution)/shard_map/reduce_first_kernel/pallas_call | solution.py:577
  292.2 4.5 %mixed_grad_kernel.1.refs_4_.refs_3_ = bf16[4,208,2304]{2,1,0:T(8,128)(2,1)} custom-call(bf16[4,208,768]{2,1,0:T(8,128)(2,1)} %get-tuple-element.161.refs_4_.refs_0_, bf16[2,4,208,768]{3,2,1,0:T(8,128)(2,1)} %get-tuple-element.162.refs_1_, bf16[2,4,208,768]{3,2,1,0:T(8,128)(2,1)} %collective-permute-done.34.refs_2_, ...), custom_call_target="tpu_custom_call" | custom-call | flops 3000000000 | bytes 1 | tf_op jit(solution)/shard_map/mixed_grad_kernel/pallas_call | solution.py:577
  297.6 3.9 reduce_second_kernel.4
  303.9 10.6 %time_mix_back_kernel.1 = (f32[4,196,768]{2,1,0:T(8,128)}, f32[8,768]{1,0:T(8,128)}) custom-call(s32[5]{0:T(128)} %stack.27.refs_0_, bf16[4,208,768]{2,1,0:T(8,128)(2,1)} %copy-done, f32[128,768]{1,0:T(8,128)} %turn_kernel.1.refs_3_.refs_2_.refs_7_, bf16[4,208,2304]{2,1,0:T(8,128)(2,1)} %mixed_grad_kernel.1.refs_4_.refs_3_, ...), custom_call_target="tpu_custom_call" | custom-call | flops 4000000000 | bytes 1 | tf_op jit(solution)/shard_map/time_mix_back_kernel/pallas_call | solution.py:577
  323.4 8.4 %time_outer_kernel.1 = (bf16[16,24,2432]{2,1,0:T(8,128)(2,1)}, bf16[16,24,2432]{2,1,0:T(8,128)(2,1)}) custom-call(s32[1]{0:T(128)} %bitcast.refs_0_, bf16[832,768]{1,0:T(8,128)(2,1)} %bitcast.50, bf16[832,2304]{1,0:T(8,128)(2,1)} %bitcast.54, f32[768,128]{1,0:T(8,128)} %sums_kernel.1.refs_3_, bf16[24,3840]{1,0:T(8,128)(2,1)} %get-tuple-element.184.refs_4_), custom_call_target="tpu_custom_call" | custom-call | flops 8000000000 | bytes 1 | tf_op jit(solution)/shard_map/time_outer_kernel/pallas_call | solution.py:577
  336.1 4.3 %reduce_first_kernel.5 = (bf16[2,24,2432]{2,1,0:T(8,128)(2,1)}, bf16[2,24,2432]{2,1,0:T(8,128)(2,1)}, bf16[4,24,2432]{2,1,0:T(8,128)(2,1)}, bf16[4,24,2432]{2,1,0:T(8,128)(2,1)}, bf16[4,24,2432]{2,1,0:T(8,128)(2,1)}) custom-call(s32[5]{0:T(128)} %stack.27.refs_0_, bf16[4,4,24,2432]{3,2,1,0:T(8,128)(2,1)} %bitcast.57, bf16[4,4,24,2432]{3,2,1,0:T(8,128)(2,1)} %bitcast.33.refs_2_), custom_call_target="tpu_custom_call" | custom-call | flops 20000000000 | bytes 1 | tf_op jit(solution)/shard_map/reduce_first_kernel/pallas_call | solution.py:577
  342.2 6.2 %collective-permute-done.47.refs_2_ = bf16[2,24,2432]{2,1,0:T(8,128)(2,1)S(1)} collective-permute-done((bf16[2,24,2432]{2,1,0:T(8,128)(2,1)}, bf16[2,24,2432]{2,1,0:T(8,128)(2,1)S(1)}, u32[]{:S(2)}, u32[]{:S(2)}) %collective-permute-start.47) | collective-permute-done | bytes 233504 | tf_op jit(solution)/shard_map/ppermute | solution.py:808
  349.8 3.8 reduce_second_kernel.5
  373.0 8.2 %collective-permute-done.55.refs_2_ = bf16[24,3840]{1,0:T(8,128)(2,1)S(1)} collective-permute-done((bf16[24,3840]{1,0:T(8,128)(2,1)}, bf16[24,3840]{1,0:T(8,128)(2,1)S(1)}, u32[]{:S(2)}, u32[]{:S(2)}) %collective-permute-start.55) | collective-permute-done | bytes 184352 | tf_op jit(solution)/shard_map/ppermute | solution.py:808
  (272 shorter events, 152.3 us)
Async XLA Ops:
  20.8 33.3 %collective-permute-start.8 = (bf16[4,208,768]{2,1,0:T(8,128)(2,1)}, bf16[4,208,768]{2,1,0:T(8,128)(2,1)S(1)}, u32[]{:S(2)}, u32[]{:S(2)}) collective-permute-start(bf16[4,208,768]{2,1,0:T(8,128)(2,1)} %shard_map.257), channel_id=1, source_target_pairs={{0,1},{1,0},{2,3},{3,2},{4,5},{5,4},{6,7},{7,6},{8,9},{9,8},{10,11... | collective-permute-start | bytes 3833864 | tf_op jit(solution)/shard_map/ppermute | solution.py:812
  58.2 21.2 %collective-permute-start.13 = (bf16[4,48,1920]{2,1,0:T(8,128)(2,1)}, bf16[4,48,1920]{2,1,0:T(8,128)(2,1)S(1)}, u32[]{:S(2)}, u32[]{:S(2)}) collective-permute-start(bf16[4,48,1920]{2,1,0:T(8,128)(2,1)} %shard_map.259.refs_1_.refs_6_), channel_id=1, source_target_pairs={{0,2},{2,0},{4,6},{6,4},{8,10},{10,8},{12,14},{14,12},{16,18},{18,... | collective-permute-start | bytes 2211848 | tf_op jit(solution)/shard_map/ppermute | solution.py:808
  59.5 19.9 %collective-permute-start.14 = (bf16[4,48,1920]{2,1,0:T(8,128)(2,1)}, bf16[4,48,1920]{2,1,0:T(8,128)(2,1)}, u32[]{:S(2)}, u32[]{:S(2)}) collective-permute-start(bf16[4,48,1920]{2,1,0:T(8,128)(2,1)} %shard_map.259.refs_1_.refs_6_), channel_id=1, source_target_pairs={{0,4},{2,6},{4,0},{6,2},{8,12},{10,14},{12,8},{14,10},{16,20},{18,... | collective-permute-start | bytes 2211848 | tf_op jit(solution)/shard_map/ppermute | solution.py:808
  60.0 24.4 %collective-permute-start.17 = (bf16[192,768]{1,0:T(8,128)(2,1)}, bf16[192,768]{1,0:T(8,128)(2,1)S(1)}, u32[]{:S(2)}, u32[]{:S(2)}) collective-permute-start(bf16[192,768]{1,0:T(8,128)(2,1)} %shard_map.260.refs_7_.refs_1_), channel_id=1, source_target_pairs={{0,8},{2,10},{4,12},{6,14},{8,0},{10,2},{12,4},{14,6},{16,24},{18,... | collective-permute-start | bytes 884744 | tf_op jit(solution)/shard_map/ppermute | solution.py:808
  60.8 23.7 %collective-permute-start.18 = (bf16[192,768]{1,0:T(8,128)(2,1)}, bf16[192,768]{1,0:T(8,128)(2,1)S(1)}, u32[]{:S(2)}, u32[]{:S(2)}) collective-permute-start(bf16[192,768]{1,0:T(8,128)(2,1)} %shard_map.260.refs_7_.refs_1_), channel_id=1, source_target_pairs={{0,16},{2,18},{4,20},{6,22},{8,24},{10,26},{12,28},{14,30},{16,0},... | collective-permute-start | bytes 884744 | tf_op jit(solution)/shard_map/ppermute | solution.py:808
  64.9 19.6 %collective-permute-start.19 = (bf16[192,768]{1,0:T(8,128)(2,1)S(1)}, bf16[192,768]{1,0:T(8,128)(2,1)}, u32[]{:S(2)}, u32[]{:S(2)}) collective-permute-start(bf16[192,768]{1,0:T(8,128)(2,1)S(1)} %copy-done.8), channel_id=1, source_target_pairs={{0,24},{2,26},{4,28},{6,30},{8,16},{10,18},{12,20},{14,22},{16,8},... | collective-permute-start | bytes 884744 | tf_op jit(solution)/shard_map/ppermute | solution.py:808
  97.6 31.3 %collective-permute-start.22 = (bf16[4,192,768]{2,1,0:T(8,128)(2,1)}, bf16[4,192,768]{2,1,0:T(8,128)(2,1)S(1)}, u32[]{:S(2)}, u32[]{:S(2)}) collective-permute-start(bf16[4,192,768]{2,1,0:T(8,128)(2,1)} %shard_map.261.refs_9_.source), channel_id=1, source_target_pairs={{0,2},{2,0},{4,6},{6,4},{8,10},{10,8},{12,14},{14,12},{16,18},{18,... | collective-permute-start | bytes 3538952 | tf_op jit(solution)/shard_map/ppermute | solution.py:808
  98.3 30.6 %collective-permute-start.23 = (bf16[4,192,768]{2,1,0:T(8,128)(2,1)}, bf16[4,192,768]{2,1,0:T(8,128)(2,1)S(1)}, u32[]{:S(2)}, u32[]{:S(2)}) collective-permute-start(bf16[4,192,768]{2,1,0:T(8,128)(2,1)} %shard_map.261.refs_9_.source), channel_id=1, source_target_pairs={{0,4},{2,6},{4,0},{6,2},{8,12},{10,14},{12,8},{14,10},{16,20},{18,... | collective-permute-start | bytes 3538952 | tf_op jit(solution)/shard_map/ppermute | solution.py:808
  134.4 19.7 %collective-permute-start.28 = (bf16[4,192,768]{2,1,0:T(8,128)(2,1)}, bf16[4,192,768]{2,1,0:T(8,128)(2,1)S(1)}, u32[]{:S(2)}, u32[]{:S(2)}) collective-permute-start(bf16[4,192,768]{2,1,0:T(8,128)(2,1)} %shard_map.264.refs_11_), channel_id=1, source_target_pairs={{0,1},{1,0},{2,3},{3,2},{4,5},{5,4},{6,7},{7,6},{8,9},{9,8},{10,11... | collective-permute-start | bytes 3538952 | tf_op jit(solution)/shard_map/ppermute | solution.py:812
  134.5 19.6 %collective-permute-start.27 = (bf16[4,192,768]{2,1,0:T(8,128)(2,1)}, bf16[4,192,768]{2,1,0:T(8,128)(2,1)}, u32[]{:S(2)}, u32[]{:S(2)}) collective-permute-start(bf16[4,192,768]{2,1,0:T(8,128)(2,1)} %shard_map.263.refs_10_), channel_id=1, source_target_pairs={{0,1},{1,0},{2,3},{3,2},{4,5},{5,4},{6,7},{7,6},{8,9},{9,8},{10,11... | collective-permute-start | bytes 3538952 | tf_op jit(solution)/shard_map/ppermute | solution.py:812
  135.7 18.4 %collective-permute-start.26 = (bf16[4,192,768]{2,1,0:T(8,128)(2,1)S(1)}, bf16[4,192,768]{2,1,0:T(8,128)(2,1)}, u32[]{:S(2)}, u32[]{:S(2)}) collective-permute-start(bf16[4,192,768]{2,1,0:T(8,128)(2,1)S(1)} %copy-done.2), channel_id=1, source_target_pairs={{0,1},{1,0},{2,3},{3,2},{4,5},{5,4},{6,7},{7,6},{8,9},{9,8},{10,11... | collective-permute-start | bytes 3538952 | tf_op jit(solution)/shard_map/ppermute | solution.py:812
  220.7 18.0 %collective-permute-start.32 = (bf16[2,192,768]{2,1,0:T(8,128)(2,1)}, bf16[2,192,768]{2,1,0:T(8,128)(2,1)S(1)}, u32[]{:S(2)}, u32[]{:S(2)}) collective-permute-start(bf16[2,192,768]{2,1,0:T(8,128)(2,1)} %get-tuple-element.148.refs_16_), channel_id=1, source_target_pairs={{0,4},{2,6},{4,0},{6,2},{8,12},{10,14},{12,8},{14,10},{16,20},{18,... | collective-permute-start | bytes 1769480 | tf_op jit(solution)/shard_map/ppermute | solution.py:808
  244.0 30.9 %collective-permute-start.36 = (bf16[4,192,768]{2,1,0:T(8,128)(2,1)}, bf16[4,192,768]{2,1,0:T(8,128)(2,1)}, u32[]{:S(2)}, u32[]{:S(2)}) collective-permute-start(bf16[4,192,768]{2,1,0:T(8,128)(2,1)} %get-tuple-element.154.refs_7_.refs_5_), channel_id=1, source_target_pairs={{0,2},{2,0},{4,6},{6,4},{8,10},{10,8},{12,14},{14,12},{16,18},{18,... | collective-permute-start | bytes 3538952 | tf_op jit(solution)/shard_map/ppermute | solution.py:808
  245.3 29.6 %collective-permute-start.37 = (bf16[4,192,768]{2,1,0:T(8,128)(2,1)}, bf16[4,192,768]{2,1,0:T(8,128)(2,1)}, u32[]{:S(2)}, u32[]{:S(2)}) collective-permute-start(bf16[4,192,768]{2,1,0:T(8,128)(2,1)} %get-tuple-element.155.refs_8_.refs_6_), channel_id=1, source_target_pairs={{0,4},{2,6},{4,0},{6,2},{8,12},{10,14},{12,8},{14,10},{16,20},{18,... | collective-permute-start | bytes 3538952 | tf_op jit(solution)/shard_map/ppermute | solution.py:808
  258.3 20.0 %collective-permute-start.35 = (bf16[16,24,3840]{2,1,0:T(8,128)(2,1)}, bf16[16,24,3840]{2,1,0:T(8,128)(2,1)S(1)}, u32[]{:S(2)}, u32[]{:S(2)}) collective-permute-start(bf16[16,24,3840]{2,1,0:T(8,128)(2,1)} %get-tuple-element.160.refs_7_), channel_id=1, source_target_pairs={{0,1},{1,0},{2,3},{3,2},{4,5},{5,4},{6,7},{7,6},{8,9},{9,8},{10,11... | collective-permute-start | bytes 8847368 | tf_op jit(solution)/shard_map/ppermute | solution.py:812
  287.8 29.0 %collective-permute-start.43 = (bf16[192,768]{1,0:T(8,128)(2,1)}, bf16[192,768]{1,0:T(8,128)(2,1)S(1)}, u32[]{:S(2)}, u32[]{:S(2)}) collective-permute-start(bf16[192,768]{1,0:T(8,128)(2,1)} %get-tuple-element.166.refs_3_.refs_7_), channel_id=1, source_target_pairs={{0,8},{2,10},{4,12},{6,14},{8,0},{10,2},{12,4},{14,6},{16,24},{18,... | collective-permute-start | bytes 884744 | tf_op jit(solution)/shard_map/ppermute | solution.py:808
  288.9 27.9 %collective-permute-start.44 = (bf16[192,768]{1,0:T(8,128)(2,1)}, bf16[192,768]{1,0:T(8,128)(2,1)S(1)}, u32[]{:S(2)}, u32[]{:S(2)}) collective-permute-start(bf16[192,768]{1,0:T(8,128)(2,1)} %get-tuple-element.181), channel_id=1, source_target_pairs={{0,16},{2,18},{4,20},{6,22},{8,24},{10,26},{12,28},{14,30},{16,0},... | collective-permute-start | bytes 884744 | tf_op jit(solution)/shard_map/ppermute | solution.py:808
  290.7 26.2 %collective-permute-start.45 = (bf16[192,768]{1,0:T(8,128)(2,1)S(1)}, bf16[192,768]{1,0:T(8,128)(2,1)S(1)}, u32[]{:S(2)}, u32[]{:S(2)}) collective-permute-start(bf16[192,768]{1,0:T(8,128)(2,1)S(1)} %copy-done.31), channel_id=1, source_target_pairs={{0,24},{2,26},{4,28},{6,30},{8,16},{10,18},{12,20},{14,22},{16,8},... | collective-permute-start | bytes 884744 | tf_op jit(solution)/shard_map/ppermute | solution.py:808
  301.5 18.3 %collective-permute-start.41 = (bf16[4,24,3840]{2,1,0:T(8,128)(2,1)}, bf16[4,24,3840]{2,1,0:T(8,128)(2,1)S(1)}, u32[]{:S(2)}, u32[]{:S(2)}) collective-permute-start(bf16[4,24,3840]{2,1,0:T(8,128)(2,1)} %get-tuple-element.173.refs_8_), channel_id=1, source_target_pairs={{0,2},{2,0},{4,6},{6,4},{8,10},{10,8},{12,14},{14,12},{16,18},{18,... | collective-permute-start | bytes 2211848 | tf_op jit(solution)/shard_map/ppermute | solution.py:808
  302.9 17.0 %collective-permute-start.42 = (bf16[4,24,3840]{2,1,0:T(8,128)(2,1)}, bf16[4,24,3840]{2,1,0:T(8,128)(2,1)S(1)}, u32[]{:S(2)}, u32[]{:S(2)}) collective-permute-start(bf16[4,24,3840]{2,1,0:T(8,128)(2,1)} %get-tuple-element.174.refs_9_), channel_id=1, source_target_pairs={{0,4},{2,6},{4,0},{6,2},{8,12},{10,14},{12,8},{14,10},{16,20},{18,... | collective-permute-start | bytes 2211848 | tf_op jit(solution)/shard_map/ppermute | solution.py:808
  334.7 20.5 %collective-permute-start.40 = (f32[8,768]{1,0:T(8,128)S(1)}, f32[8,768]{1,0:T(8,128)S(1)}, u32[]{:S(2)}, u32[]{:S(2)}) collective-permute-start(f32[8,768]{1,0:T(8,128)S(1)} %copy-done.15), channel_id=1, source_target_pairs={{0,1},{1,0},{2,3},{3,2},{4,5},{5,4},{6,7},{7,6},{8,9},{9,8},{10,11... | collective-permute-start | bytes 73736 | tf_op jit(solution)/shard_map/ppermute | solution.py:812
  360.7 20.5 %collective-permute-start.55 = (bf16[24,3840]{1,0:T(8,128)(2,1)}, bf16[24,3840]{1,0:T(8,128)(2,1)S(1)}, u32[]{:S(2)}, u32[]{:S(2)}) collective-permute-start(bf16[24,3840]{1,0:T(8,128)(2,1)} %get-tuple-element.200), channel_id=1, source_target_pairs={{0,16},{2,18},{4,20},{6,22},{8,24},{10,26},{12,28},{14,30},{16,0},... | collective-permute-start | bytes 552968 | tf_op jit(solution)/shard_map/ppermute | solution.py:808
  362.5 18.7 %collective-permute-start.56 = (bf16[24,3840]{1,0:T(8,128)(2,1)S(1)}, bf16[24,3840]{1,0:T(8,128)(2,1)S(1)}, u32[]{:S(2)}, u32[]{:S(2)}) collective-permute-start(bf16[24,3840]{1,0:T(8,128)(2,1)S(1)} %copy-done.42), channel_id=1, source_target_pairs={{0,24},{2,26},{4,28},{6,30},{8,16},{10,18},{12,20},{14,22},{16,8},... | collective-permute-start | bytes 552968 | tf_op jit(solution)/shard_map/ppermute | solution.py:808
  369.7 17.4 %collective-permute-start.52 = (bf16[24,2432]{1,0:T(8,128)(2,1)}, bf16[24,2432]{1,0:T(8,128)(2,1)S(1)}, u32[]{:S(2)}, u32[]{:S(2)}) collective-permute-start(bf16[24,2432]{1,0:T(8,128)(2,1)} %get-tuple-element.196), channel_id=1, source_target_pairs={{0,16},{2,18},{4,20},{6,22},{8,24},{10,26},{12,28},{14,30},{16,0},... | collective-permute-start | bytes 350216 | tf_op jit(solution)/shard_map/ppermute | solution.py:808
  (89 other events, 504.5 us)
where the time goes:
time: 396 us; the launch traced here: 392 us
  Pallas kernels  233 us (59%)
  starting transfers between devices  58.1 us (15%)
  waiting for transfers between devices  57.9 us (15%)
  local copies, waits for them, and re-layouts  34.9 us (9%)
  other arithmetic  5.32 us (1%)
    pallas_call x35, Pallas kernels, call(): pl.pallas_call(inner, **common)  233 us
    ppermute x42, starting transfers between devices, clip_swap(): return lax.ppermute(values, 'clip', [(i, i ^ bits) for i in range(count)])  55.1 us
    ppermute x42, waiting for transfers between devices, clip_swap(): return lax.ppermute(values, 'clip', [(i, i ^ bits) for i in range(count)])  53 us
    unnamed x113, local copies, waits for them, and re-layouts  23.2 us
  transfers between devices with their start and end apart: 58, of which 17 were waited for; matrix products, arithmetic and copies ran while one was open for 5% of the time, Pallas kernels for 40%

commit v1 on v0

--- a/solution.py
+++ b/solution.py
@@ -14,7 +14,7 @@
 LANES = 128
 BLOCKS = 16
 RATE = 1e9
-VMEM_BYTES = 60 * 1024 * 1024
+VMEM_BYTES = 63 * 1024 * 1024
 
 
 def nn(left, right):

time: 396 us -> 392 us (0.990)
  local copies, waits for them, and re-layouts: 34.9 us -> 29.4 us
    unnamed x113 -> x69, local copies, waits for them, and re-layouts: 23.2 us -> 17 us
  transfers between devices with their start and end apart: 58 -> 58, of which waited for: 17 -> 18; matrix products, arithmetic and copies ran while one was open for 5% -> 6% of each run, Pallas kernels for 40% -> 40%
where the time goes in v1:
time: 392 us; the launch traced here: 387 us
  Pallas kernels  233 us (59%)
  starting transfers between devices  59.2 us (15%)
  waiting for transfers between devices  57.8 us (15%)
  local copies, waits for them, and re-layouts  29.4 us (8%)
  other arithmetic  5.7 us (1%)
    pallas_call x35, Pallas kernels, call(): pl.pallas_call(inner, **common)  233 us
    ppermute x42, starting transfers between devices, clip_swap(): return lax.ppermute(values, 'clip', [(i, i ^ bits) for i in range(count)])  56.3 us
    ppermute x42, waiting for transfers between devices, clip_swap(): return lax.ppermute(values, 'clip', [(i, i ^ bits) for i in range(count)])  54.5 us
    unnamed x69, local copies, waits for them, and re-layouts  17 us
  transfers between devices with their start and end apart: 58, of which 18 were waited for; matrix products, arithmetic and copies ran while one was open for 6% of the time, Pallas kernels for 40%

profile of v1, /device:TPU:0, one launch (start us, length us, event | category | flops | bytes accessed | tf_op | source)
XLA Modules:
  0.0 387.1 jit_solution(10058926632440140426)
XLA Ops:
  22.5 4.4 %collective-permute-done.2.refs_2_ = bf16[48,1280]{1,0:T(8,128)(2,1)S(1)} collective-permute-done((bf16[48,1280]{1,0:T(8,128)(2,1)}, bf16[48,1280]{1,0:T(8,128)(2,1)S(1)}, u32[]{:S(2)}, u32[]{:S(2)}) %collective-permute-start.2) | collective-permute-done | bytes 122912 | tf_op jit(solution)/shard_map/ppermute | solution.py:808
  37.2 4.3 %collective-permute-done.4.refs_0_.refs_2_ = bf16[4,48,1280]{2,1,0:T(8,128)(2,1)S(1)} collective-permute-done((bf16[4,48,1280]{2,1,0:T(8,128)(2,1)}, bf16[4,48,1280]{2,1,0:T(8,128)(2,1)S(1)}, u32[]{:S(2)}, u32[]{:S(2)}) %collective-permute-start.4) | collective-permute-done | bytes 491552 | tf_op jit(solution)/shard_map/ppermute | solution.py:808
  66.3 12.9 %time_mix_kernel.1 = (bf16[4,208,768]{2,1,0:T(8,128)(2,1)}, bf16[8,208,768]{2,1,0:T(8,128)(2,1)}, bf16[8,208,768]{2,1,0:T(8,128)(2,1)}, bf16[4,208,768]{2,1,0:T(8,128)(2,1)}) custom-call(s32[5]{0:T(128)} %stack.27.refs_0_, bf16[4,208,768]{2,1,0:T(8,128)(2,1)} %copy-done, bf16[4,208,768]{2,1,0:T(8,128)(2,1)} %collective-permute-done.8.refs_7_.refs_2_, ...), custom_call_target="tpu_custom_call" | custom-call | flops 1000000000 | bytes 1 | tf_op jit(solution)/shard_map/time_mix_kernel/pallas_call | solution.py:577
  87.3 3.8 collective-permute-done.15.refs_4_
  102.3 24.8 %attention_kernel.1 = (bf16[4,8,208,128]{3,2,1,0:T(8,128)(2,1)}, bf16[4,208,768]{2,1,0:T(8,128)(2,1)}, f32[4,208,768]{2,1,0:T(8,128)}, bf16[4,208,768]{2,1,0:T(8...) custom-call(s32[5]{0:T(128)} %stack.27.refs_0_, ...), custom_call_target="tpu_custom_call" | custom-call | flops 27000000512 | bytes 1 | tf_op jit(solution)/shard_map/attention_kernel/pallas_call | solution.py:577
  133.4 12.0 %collective-permute-done.24.refs_12_ = bf16[2,192,768]{2,1,0:T(8,128)(2,1)S(1)} collective-permute-done((bf16[2,192,768]{2,1,0:T(8,128)(2,1)}, bf16[2,192,768]{2,1,0:T(8,128)(2,1)S(1)}, u32[]{:S(2)}, u32[]{:S(2)}) %collective-permute-start.24) | collective-permute-done | bytes 589856 | tf_op jit(solution)/shard_map/ppermute | solution.py:808
  150.8 25.7 %mlp_kernel.1 = (bf16[4,196,768]{2,1,0:T(8,128)(2,1)}, f32[8,768]{1,0:T(8,128)}, bf16[4,208,768]{2,1,0:T(8,128)(2,1)}, bf16[4,208,3072]{2,1,0:T(8,128)(2,1)}, bf...) custom-call(s32[5]{0:T(128)} %stack.27.refs_0_, ...), custom_call_target="tpu_custom_call" | custom-call | flops 24999999488 | bytes 1 | tf_op jit(solution)/shard_map/mlp_kernel/pallas_call | solution.py:577
  176.5 16.2 %mlp_outer_kernel.1 = (bf16[16,192,768]{2,1,0:T(8,128)(2,1)}, bf16[16,192,768]{2,1,0:T(8,128)(2,1)}) custom-call(s32[1]{0:T(128)} %bitcast.refs_0_, bf16[832,768]{1,0:T(8,128)(2,1)} %bitcast.61, bf16[832,3072]{1,0:T(8,128)(2,1)} %bitcast.50, bf16[832,3072]{1,0:T(8,128)(2,1)} %bitcast.49, bf16[832,768]{1,0:T(8,128)(2,1)} %bitcast.62), custom_call_target="tpu_custom_call" | custom-call | flops 20999999488 | bytes 1 | tf_op jit(solution)/shard_map/mlp_outer_kernel/pallas_call | solution.py:577
  193.3 16.2 %space_back_kernel.2 = (bf16[4,208,768]{2,1,0:T(8,128)(2,1)}, bf16[4,208,2304]{2,1,0:T(8,128)(2,1)}, f32[4,208,768]{2,1,0:T(8,128)}, bf16[4,208,768]{2,1,0:T(8,1...) custom-call(s32[5]{0:T(128)} %stack.27.refs_0_, f32[4,208,768]{2,1,0:T(8,128)} %get-tuple-element.131.refs_1_.refs_2_, ...), custom_call_target="tpu_custom_call" | custom-call | flops 15000000512 | bytes 1 | tf_op jit(solution)/shard_map/space_back_kernel/pallas_call | solution.py:577
  209.5 6.8 %reduce_first_kernel.3 = (bf16[2,192,768]{2,1,0:T(8,128)(2,1)}, bf16[2,192,768]{2,1,0:T(8,128)(2,1)}, bf16[4,192,768]{2,1,0:T(8,128)(2,1)}, bf16[4,192,768]{2,1,0:T(8,128)(2,1)}, bf16[4,192,768]{2,1,0:T(8,128)(2,1)}) custom-call(s32[5]{0:T(128)} %stack.27.refs_0_, bf16[4,4,192,768]{3,2,1,0:T(8,128)(2,1)} %bitcast.51, ...), custom_call_target="tpu_custom_call" | custom-call | flops 20000000000 | bytes 1 | tf_op jit(solution)/shard_map/reduce_first_kernel/pallas_call | solution.py:577
  219.0 16.2 %space_back_kernel.3 = (bf16[4,208,768]{2,1,0:T(8,128)(2,1)}, bf16[4,208,2304]{2,1,0:T(8,128)(2,1)}, f32[4,208,768]{2,1,0:T(8,128)}, bf16[4,208,768]{2,1,0:T(8,1...) custom-call(s32[5]{0:T(128)} %stack.27.refs_0_, ...), custom_call_target="tpu_custom_call", output_to_operand_aliasing={{0}: (11, {}), {1}: (12, {}), {2}: (13, {}), {3}: (14, {}),... | custom-call | flops 15000000512 | bytes 1 | tf_op jit(solution)/shard_map/space_back_kernel/pallas_call | solution.py:577
  236.2 4.2 %reduce_second_kernel.3 = (bf16[4,192,768]{2,1,0:T(8,128)(2,1)}, bf16[4,192,768]{2,1,0:T(8,128)(2,1)}) custom-call(bf16[4,192,768]{2,1,0:T(8,128)(2,1)} %get-tuple-element.151.refs_0_, bf16[4,192,768]{2,1,0:T(8,128)(2,1)} %get-tuple-element.152.refs_1_, bf16[2,192,768]{2,1,0:T(8,128)(2,1)} %copy-done.13, ...), custom_call_target="tpu_custom_call" | custom-call | flops 20000000000 | bytes 1 | tf_op jit(solution)/shard_map/reduce_second_kernel/pallas_call | solution.py:577
  241.9 12.0 %space_outer_kernel.1 = (bf16[16,24,3840]{2,1,0:T(8,128)(2,1)}, bf16[16,24,3840]{2,1,0:T(8,128)(2,1)}) custom-call(s32[1]{0:T(128)} %bitcast.refs_0_, bf16[832,768]{1,0:T(8,128)(2,1)} %bitcast.57, bf16[832,2304]{1,0:T(8,128)(2,1)} %bitcast.53, bf16[832,768]{1,0:T(8,128)(2,1)} %bitcast.58, bf16[832,768]{1,0:T(8,128)(2,1)} %bitcast.59, ...), custom_call_target="tpu_custom_call" | custom-call | flops 12000000000 | bytes 1 | tf_op jit(solution)/shard_map/space_outer_kernel/pallas_call | solution.py:577
  253.9 16.1 %time_back_kernel.1 = (bf16[4,208,768]{2,1,0:T(8,128)(2,1)}, bf16[2,4,208,768]{3,2,1,0:T(8,128)(2,1)}, bf16[2,4,208,768]{3,2,1,0:T(8,128)(2,1)}) custom-call(bf16[4,208,768]{2,1,0:T(8,128)(2,1)} %get-tuple-element.119.refs_2_.refs_5_.refs_3_.refs_0_, bf16[8,208,768]{2,1,0:T(8,128)(2,1)} %get-tuple-element.120.refs_4_.refs_1_, ...), custom_call_target="tpu_custom_call" | custom-call | flops 19000000512 | bytes 1 | tf_op jit(solution)/shard_map/time_back_kernel/pallas_call | solution.py:577
  273.8 5.1 %reduce_first_kernel.4 = (bf16[2,24,3840]{2,1,0:T(8,128)(2,1)}, bf16[2,24,3840]{2,1,0:T(8,128)(2,1)}, bf16[4,24,3840]{2,1,0:T(8,128)(2,1)}, bf16[4,24,3840]{2,1,0:T(8,128)(2,1)}, bf16[4,24,3840]{2,1,0:T(8,128)(2,1)}) custom-call(s32[5]{0:T(128)} %stack.27.refs_0_, bf16[4,4,24,3840]{3,2,1,0:T(8,128)(2,1)} %bitcast.54, ...), custom_call_target="tpu_custom_call" | custom-call | flops 20000000000 | bytes 1 | tf_op jit(solution)/shard_map/reduce_first_kernel/pallas_call | solution.py:577
  287.1 4.5 %mixed_grad_kernel.1.refs_4_.refs_3_ = bf16[4,208,2304]{2,1,0:T(8,128)(2,1)} custom-call(bf16[4,208,768]{2,1,0:T(8,128)(2,1)} %get-tuple-element.161.refs_4_.refs_0_, bf16[2,4,208,768]{3,2,1,0:T(8,128)(2,1)} %get-tuple-element.162.refs_1_, bf16[2,4,208,768]{3,2,1,0:T(8,128)(2,1)} %collective-permute-done.34.refs_2_, ...), custom_call_target="tpu_custom_call" | custom-call | flops 3000000000 | bytes 1 | tf_op jit(solution)/shard_map/mixed_grad_kernel/pallas_call | solution.py:577
  292.5 3.9 %reduce_second_kernel.4 = (bf16[4,24,3840]{2,1,0:T(8,128)(2,1)}, bf16[4,24,3840]{2,1,0:T(8,128)(2,1)}) custom-call(bf16[4,24,3840]{2,1,0:T(8,128)(2,1)} %get-tuple-element.169.refs_0_, bf16[4,24,3840]{2,1,0:T(8,128)(2,1)} %get-tuple-element.170.refs_1_, bf16[2,24,3840]{2,1,0:T(8,128)(2,1)} %copy-done.15, bf16[2,24,3840]{2,1,0:T(8,128)(2,1)} %copy-done.16, ...), custom_call_target="tpu_custom_call" | custom-call | flops 20000000000 | bytes 1 | tf_op jit(solution)/shard_map/reduce_second_kernel/pallas_call | solution.py:577
  297.8 10.7 %time_mix_back_kernel.1 = (f32[4,196,768]{2,1,0:T(8,128)}, f32[8,768]{1,0:T(8,128)}) custom-call(s32[5]{0:T(128)} %stack.27.refs_0_, bf16[4,208,768]{2,1,0:T(8,128)(2,1)} %copy-done, f32[128,768]{1,0:T(8,128)} %turn_kernel.1.refs_3_.refs_2_.refs_7_, bf16[4,208,2304]{2,1,0:T(8,128)(2,1)} %mixed_grad_kernel.1.refs_4_.refs_3_, ...), custom_call_target="tpu_custom_call" | custom-call | flops 4000000000 | bytes 1 | tf_op jit(solution)/shard_map/time_mix_back_kernel/pallas_call | solution.py:577
  317.0 8.3 %time_outer_kernel.1 = (bf16[16,24,2432]{2,1,0:T(8,128)(2,1)}, bf16[16,24,2432]{2,1,0:T(8,128)(2,1)}) custom-call(s32[1]{0:T(128)} %bitcast.refs_0_, bf16[832,768]{1,0:T(8,128)(2,1)} %bitcast.48, bf16[832,2304]{1,0:T(8,128)(2,1)} %bitcast.52, f32[768,128]{1,0:T(8,128)} %sums_kernel.1.refs_3_, bf16[24,3840]{1,0:T(8,128)(2,1)} %get-tuple-element.184.refs_4_), custom_call_target="tpu_custom_call" | custom-call | flops 8000000000 | bytes 1 | tf_op jit(solution)/shard_map/time_outer_kernel/pallas_call | solution.py:577
  331.1 4.3 %reduce_first_kernel.5 = (bf16[2,24,2432]{2,1,0:T(8,128)(2,1)}, bf16[2,24,2432]{2,1,0:T(8,128)(2,1)}, bf16[4,24,2432]{2,1,0:T(8,128)(2,1)}, bf16[4,24,2432]{2,1,0:T(8,128)(2,1)}, bf16[4,24,2432]{2,1,0:T(8,128)(2,1)}) custom-call(s32[5]{0:T(128)} %stack.27.refs_0_, bf16[4,4,24,2432]{3,2,1,0:T(8,128)(2,1)} %bitcast.55, bf16[4,4,24,2432]{3,2,1,0:T(8,128)(2,1)} %bitcast.47), custom_call_target="tpu_custom_call" | custom-call | flops 20000000000 | bytes 1 | tf_op jit(solution)/shard_map/reduce_first_kernel/pallas_call | solution.py:577
  337.5 5.8 %collective-permute-done.47.refs_2_ = bf16[2,24,2432]{2,1,0:T(8,128)(2,1)S(1)} collective-permute-done((bf16[2,24,2432]{2,1,0:T(8,128)(2,1)}, bf16[2,24,2432]{2,1,0:T(8,128)(2,1)S(1)}, u32[]{:S(2)}, u32[]{:S(2)}) %collective-permute-start.47) | collective-permute-done | bytes 233504 | tf_op jit(solution)/shard_map/ppermute | solution.py:808
  351.1 4.1 %copy.53 = f32[1,4,196,768]{3,1,2,0:T(4,128)} copy(f32[1,4,196,768]{3,2,1,0:T(8,128)} %bitcast.44) | data formatting | bytes 4816896
  367.1 7.6 %collective-permute-done.55.refs_2_ = bf16[24,3840]{1,0:T(8,128)(2,1)S(1)} collective-permute-done((bf16[24,3840]{1,0:T(8,128)(2,1)S(1)}, bf16[24,3840]{1,0:T(8,128)(2,1)S(1)}, u32[]{:S(2)}, u32[]{:S(2)}) %collective-permute-start.55) | collective-permute-done | bytes 184352 | tf_op jit(solution)/shard_map/ppermute | solution.py:808
  377.4 6.0 %collective-permute-done.52.refs_2_ = bf16[24,2432]{1,0:T(8,128)(2,1)} collective-permute-done((bf16[24,2432]{1,0:T(8,128)(2,1)}, bf16[24,2432]{1,0:T(8,128)(2,1)}, u32[]{:S(2)}, u32[]{:S(2)}) %collective-permute-start.52) | collective-permute-done | bytes 116768 | tf_op jit(solution)/shard_map/ppermute | solution.py:808
  (228 shorter events, 149.2 us)
Async XLA Ops:
  22.5 32.9 %collective-permute-start.8 = (bf16[4,208,768]{2,1,0:T(8,128)(2,1)}, bf16[4,208,768]{2,1,0:T(8,128)(2,1)}, u32[]{:S(2)}, u32[]{:S(2)}) collective-permute-start(bf16[4,208,768]{2,1,0:T(8,128)(2,1)} %shard_map.257), channel_id=1, source_target_pairs={{0,1},{1,0},{2,3},{3,2},{4,5},{5,4},{6,7},{7,6},{8,9},{9,8},{10,11... | collective-permute-start | bytes 3833864 | tf_op jit(solution)/shard_map/ppermute | solution.py:812
  58.9 20.3 %collective-permute-start.13 = (bf16[4,48,1920]{2,1,0:T(8,128)(2,1)}, bf16[4,48,1920]{2,1,0:T(8,128)(2,1)}, u32[]{:S(2)}, u32[]{:S(2)}) collective-permute-start(bf16[4,48,1920]{2,1,0:T(8,128)(2,1)} %shard_map.259.refs_1_.refs_6_), channel_id=1, source_target_pairs={{0,2},{2,0},{4,6},{6,4},{8,10},{10,8},{12,14},{14,12},{16,18},{18,... | collective-permute-start | bytes 2211848 | tf_op jit(solution)/shard_map/ppermute | solution.py:808
  59.5 19.7 %collective-permute-start.14 = (bf16[4,48,1920]{2,1,0:T(8,128)(2,1)}, bf16[4,48,1920]{2,1,0:T(8,128)(2,1)}, u32[]{:S(2)}, u32[]{:S(2)}) collective-permute-start(bf16[4,48,1920]{2,1,0:T(8,128)(2,1)} %shard_map.259.refs_1_.refs_6_), channel_id=1, source_target_pairs={{0,4},{2,6},{4,0},{6,2},{8,12},{10,14},{12,8},{14,10},{16,20},{18,... | collective-permute-start | bytes 2211848 | tf_op jit(solution)/shard_map/ppermute | solution.py:808
  60.0 24.2 %collective-permute-start.17 = (bf16[192,768]{1,0:T(8,128)(2,1)}, bf16[192,768]{1,0:T(8,128)(2,1)S(1)}, u32[]{:S(2)}, u32[]{:S(2)}) collective-permute-start(bf16[192,768]{1,0:T(8,128)(2,1)} %shard_map.260.refs_7_.refs_1_), channel_id=1, source_target_pairs={{0,8},{2,10},{4,12},{6,14},{8,0},{10,2},{12,4},{14,6},{16,24},{18,... | collective-permute-start | bytes 884744 | tf_op jit(solution)/shard_map/ppermute | solution.py:808
  60.8 23.8 %collective-permute-start.18 = (bf16[192,768]{1,0:T(8,128)(2,1)}, bf16[192,768]{1,0:T(8,128)(2,1)}, u32[]{:S(2)}, u32[]{:S(2)}) collective-permute-start(bf16[192,768]{1,0:T(8,128)(2,1)} %shard_map.260.refs_7_.refs_1_), channel_id=1, source_target_pairs={{0,16},{2,18},{4,20},{6,22},{8,24},{10,26},{12,28},{14,30},{16,0},... | collective-permute-start | bytes 884744 | tf_op jit(solution)/shard_map/ppermute | solution.py:808
  64.9 19.7 %collective-permute-start.19 = (bf16[192,768]{1,0:T(8,128)(2,1)S(1)}, bf16[192,768]{1,0:T(8,128)(2,1)}, u32[]{:S(2)}, u32[]{:S(2)}) collective-permute-start(bf16[192,768]{1,0:T(8,128)(2,1)S(1)} %copy-done.3), channel_id=1, source_target_pairs={{0,24},{2,26},{4,28},{6,30},{8,16},{10,18},{12,20},{14,22},{16,8},... | collective-permute-start | bytes 884744 | tf_op jit(solution)/shard_map/ppermute | solution.py:808
  96.0 31.3 %collective-permute-start.22 = (bf16[4,192,768]{2,1,0:T(8,128)(2,1)}, bf16[4,192,768]{2,1,0:T(8,128)(2,1)}, u32[]{:S(2)}, u32[]{:S(2)}) collective-permute-start(bf16[4,192,768]{2,1,0:T(8,128)(2,1)} %shard_map.261.refs_9_.source), channel_id=1, source_target_pairs={{0,2},{2,0},{4,6},{6,4},{8,10},{10,8},{12,14},{14,12},{16,18},{18,... | collective-permute-start | bytes 3538952 | tf_op jit(solution)/shard_map/ppermute | solution.py:808
  97.4 29.8 %collective-permute-start.23 = (bf16[4,192,768]{2,1,0:T(8,128)(2,1)}, bf16[4,192,768]{2,1,0:T(8,128)(2,1)}, u32[]{:S(2)}, u32[]{:S(2)}) collective-permute-start(bf16[4,192,768]{2,1,0:T(8,128)(2,1)} %shard_map.261.refs_9_.source), channel_id=1, source_target_pairs={{0,4},{2,6},{4,0},{6,2},{8,12},{10,14},{12,8},{14,10},{16,20},{18,... | collective-permute-start | bytes 3538952 | tf_op jit(solution)/shard_map/ppermute | solution.py:808
  130.5 19.6 %collective-permute-start.28 = (bf16[4,192,768]{2,1,0:T(8,128)(2,1)}, bf16[4,192,768]{2,1,0:T(8,128)(2,1)}, u32[]{:S(2)}, u32[]{:S(2)}) collective-permute-start(bf16[4,192,768]{2,1,0:T(8,128)(2,1)} %shard_map.264.refs_11_), channel_id=1, source_target_pairs={{0,1},{1,0},{2,3},{3,2},{4,5},{5,4},{6,7},{7,6},{8,9},{9,8},{10,11... | collective-permute-start | bytes 3538952 | tf_op jit(solution)/shard_map/ppermute | solution.py:812
  130.6 19.5 %collective-permute-start.27 = (bf16[4,192,768]{2,1,0:T(8,128)(2,1)}, bf16[4,192,768]{2,1,0:T(8,128)(2,1)}, u32[]{:S(2)}, u32[]{:S(2)}) collective-permute-start(bf16[4,192,768]{2,1,0:T(8,128)(2,1)} %shard_map.263.refs_10_), channel_id=1, source_target_pairs={{0,1},{1,0},{2,3},{3,2},{4,5},{5,4},{6,7},{7,6},{8,9},{9,8},{10,11... | collective-permute-start | bytes 3538952 | tf_op jit(solution)/shard_map/ppermute | solution.py:812
  131.8 18.3 %collective-permute-start.26 = (bf16[4,192,768]{2,1,0:T(8,128)(2,1)S(1)}, bf16[4,192,768]{2,1,0:T(8,128)(2,1)}, u32[]{:S(2)}, u32[]{:S(2)}) collective-permute-start(bf16[4,192,768]{2,1,0:T(8,128)(2,1)S(1)} %copy-done.2), channel_id=1, source_target_pairs={{0,1},{1,0},{2,3},{3,2},{4,5},{5,4},{6,7},{7,6},{8,9},{9,8},{10,11... | collective-permute-start | bytes 3538952 | tf_op jit(solution)/shard_map/ppermute | solution.py:812
  216.4 18.9 %collective-permute-start.32 = (bf16[2,192,768]{2,1,0:T(8,128)(2,1)}, bf16[2,192,768]{2,1,0:T(8,128)(2,1)S(1)}, u32[]{:S(2)}, u32[]{:S(2)}) collective-permute-start(bf16[2,192,768]{2,1,0:T(8,128)(2,1)} %get-tuple-element.148.refs_16_), channel_id=1, source_target_pairs={{0,4},{2,6},{4,0},{6,2},{8,12},{10,14},{12,8},{14,10},{16,20},{18,... | collective-permute-start | bytes 1769480 | tf_op jit(solution)/shard_map/ppermute | solution.py:808
  217.6 17.8 %collective-permute-start.33 = (bf16[2,192,768]{2,1,0:T(8,128)(2,1)}, bf16[2,192,768]{2,1,0:T(8,128)(2,1)}, u32[]{:S(2)}, u32[]{:S(2)}) collective-permute-start(bf16[2,192,768]{2,1,0:T(8,128)(2,1)} %get-tuple-element.149.refs_17_), channel_id=1, source_target_pairs={{0,2},{2,0},{4,6},{6,4},{8,10},{10,8},{12,14},{14,12},{16,18},{18,... | collective-permute-start | bytes 1769480 | tf_op jit(solution)/shard_map/ppermute | solution.py:808
  240.4 30.1 %collective-permute-start.36 = (bf16[4,192,768]{2,1,0:T(8,128)(2,1)}, bf16[4,192,768]{2,1,0:T(8,128)(2,1)}, u32[]{:S(2)}, u32[]{:S(2)}) collective-permute-start(bf16[4,192,768]{2,1,0:T(8,128)(2,1)} %get-tuple-element.154.refs_7_.refs_5_), channel_id=1, source_target_pairs={{0,2},{2,0},{4,6},{6,4},{8,10},{10,8},{12,14},{14,12},{16,18},{18,... | collective-permute-start | bytes 3538952 | tf_op jit(solution)/shard_map/ppermute | solution.py:808
  240.9 29.5 %collective-permute-start.37 = (bf16[4,192,768]{2,1,0:T(8,128)(2,1)}, bf16[4,192,768]{2,1,0:T(8,128)(2,1)}, u32[]{:S(2)}, u32[]{:S(2)}) collective-permute-start(bf16[4,192,768]{2,1,0:T(8,128)(2,1)} %get-tuple-element.155.refs_8_.refs_6_), channel_id=1, source_target_pairs={{0,4},{2,6},{4,0},{6,2},{8,12},{10,14},{12,8},{14,10},{16,20},{18,... | collective-permute-start | bytes 3538952 | tf_op jit(solution)/shard_map/ppermute | solution.py:808
  253.8 20.0 %collective-permute-start.35 = (bf16[16,24,3840]{2,1,0:T(8,128)(2,1)}, bf16[16,24,3840]{2,1,0:T(8,128)(2,1)}, u32[]{:S(2)}, u32[]{:S(2)}) collective-permute-start(bf16[16,24,3840]{2,1,0:T(8,128)(2,1)} %get-tuple-element.160.refs_7_), channel_id=1, source_target_pairs={{0,1},{1,0},{2,3},{3,2},{4,5},{5,4},{6,7},{7,6},{8,9},{9,8},{10,11... | collective-permute-start | bytes 8847368 | tf_op jit(solution)/shard_map/ppermute | solution.py:812
  282.7 28.1 %collective-permute-start.43 = (bf16[192,768]{1,0:T(8,128)(2,1)}, bf16[192,768]{1,0:T(8,128)(2,1)}, u32[]{:S(2)}, u32[]{:S(2)}) collective-permute-start(bf16[192,768]{1,0:T(8,128)(2,1)} %get-tuple-element.166.refs_3_.refs_7_), channel_id=1, source_target_pairs={{0,8},{2,10},{4,12},{6,14},{8,0},{10,2},{12,4},{14,6},{16,24},{18,... | collective-permute-start | bytes 884744 | tf_op jit(solution)/shard_map/ppermute | solution.py:808
  283.2 27.6 %collective-permute-start.44 = (bf16[192,768]{1,0:T(8,128)(2,1)}, bf16[192,768]{1,0:T(8,128)(2,1)}, u32[]{:S(2)}, u32[]{:S(2)}) collective-permute-start(bf16[192,768]{1,0:T(8,128)(2,1)} %get-tuple-element.181), channel_id=1, source_target_pairs={{0,16},{2,18},{4,20},{6,22},{8,24},{10,26},{12,28},{14,30},{16,0},... | collective-permute-start | bytes 884744 | tf_op jit(solution)/shard_map/ppermute | solution.py:808
  285.5 25.3 %collective-permute-start.45 = (bf16[192,768]{1,0:T(8,128)(2,1)}, bf16[192,768]{1,0:T(8,128)(2,1)}, u32[]{:S(2)}, u32[]{:S(2)}) collective-permute-start(bf16[192,768]{1,0:T(8,128)(2,1)} %get-tuple-element.182), channel_id=1, source_target_pairs={{0,24},{2,26},{4,28},{6,30},{8,16},{10,18},{12,20},{14,22},{16,8},... | collective-permute-start | bytes 884744 | tf_op jit(solution)/shard_map/ppermute | solution.py:808
  329.4 20.4 %collective-permute-start.40 = (f32[8,768]{1,0:T(8,128)S(1)}, f32[8,768]{1,0:T(8,128)S(1)}, u32[]{:S(2)}, u32[]{:S(2)}) collective-permute-start(f32[8,768]{1,0:T(8,128)S(1)} %copy-done.8), channel_id=1, source_target_pairs={{0,1},{1,0},{2,3},{3,2},{4,5},{5,4},{6,7},{7,6},{8,9},{9,8},{10,11... | collective-permute-start | bytes 73736 | tf_op jit(solution)/shard_map/ppermute | solution.py:812
  337.5 17.7 %collective-permute-start.57 = (f32[24,1536]{1,0:T(8,128)S(1)}, f32[24,1536]{1,0:T(8,128)S(1)}, u32[]{:S(2)}, u32[]{:S(2)}) collective-permute-start(f32[24,1536]{1,0:T(8,128)S(1)} %get-tuple-element.239), channel_id=1, source_target_pairs={{0,1},{1,0},{2,3},{3,2},{4,5},{5,4},{6,7},{7,6},{8,9},{9,8},{10,11... | collective-permute-start | bytes 442376 | tf_op jit(solution)/shard_map/ppermute | solution.py:812
  356.8 17.9 %collective-permute-start.55 = (bf16[24,3840]{1,0:T(8,128)(2,1)S(1)}, bf16[24,3840]{1,0:T(8,128)(2,1)S(1)}, u32[]{:S(2)}, u32[]{:S(2)}) collective-permute-start(bf16[24,3840]{1,0:T(8,128)(2,1)S(1)} %copy-done.24), channel_id=1, source_target_pairs={{0,16},{2,18},{4,20},{6,22},{8,24},{10,26},{12,28},{14,30},{16,0},... | collective-permute-start | bytes 552968 | tf_op jit(solution)/shard_map/ppermute | solution.py:808
  363.4 20.0 %collective-permute-start.52 = (bf16[24,2432]{1,0:T(8,128)(2,1)}, bf16[24,2432]{1,0:T(8,128)(2,1)}, u32[]{:S(2)}, u32[]{:S(2)}) collective-permute-start(bf16[24,2432]{1,0:T(8,128)(2,1)} %get-tuple-element.196), channel_id=1, source_target_pairs={{0,16},{2,18},{4,20},{6,22},{8,24},{10,26},{12,28},{14,30},{16,0},... | collective-permute-start | bytes 350216 | tf_op jit(solution)/shard_map/ppermute | solution.py:808
  365.5 17.9 %collective-permute-start.53 = (bf16[24,2432]{1,0:T(8,128)(2,1)}, bf16[24,2432]{1,0:T(8,128)(2,1)}, u32[]{:S(2)}, u32[]{:S(2)}) collective-permute-start(bf16[24,2432]{1,0:T(8,128)(2,1)} %get-tuple-element.197), channel_id=1, source_target_pairs={{0,24},{2,26},{4,28},{6,30},{8,16},{10,18},{12,20},{14,22},{16,8},... | collective-permute-start | bytes 350216 | tf_op jit(solution)/shard_map/ppermute | solution.py:808
  (67 other events, 470.4 us)
